TPU v7x, 32 devices: a whole 2x2x4 slice. The times are simulated.
32 devices in a mesh: dp: 8 (over z, x), tensor: 4 (over y, core).
Axes of the slice: x: 2, y: 2, z: 4, core: 2. Of those that a mesh axis runs over, the one named last changes fastest.
Arguments:
- residual: bfloat16 [16384, 1024], P(('dp', 'tensor')), may hold values from -6 to 6
- cotangent: bfloat16 [16384, 1024], P(('dp', 'tensor')), may hold values from -6 to 6
- seq_ids: int32 [16384], P('dp'), may hold values from -1 to 15, as said below
- w_zx: bfloat16 [1024, 2, 2048], P('dp', None, 'tensor'), may hold values from -0.1875 to 0.1875
- w_bc: bfloat16 [1024, 256], P('dp'), may hold values from -0.1875 to 0.1875
- w_dt: bfloat16 [1024, 32], P('dp', 'tensor'), may hold values from -0.09375 to 0.09375
- w_out: bfloat16 [2048, 1024], P('tensor', 'dp'), may hold values from -0.125 to 0.125
- conv_weight: float32 [4, 2304], replicated, may hold values from -3 to 3
- conv_bias: float32 [2304], replicated, may hold values from -2 to 2
- dt_bias: float32 [32], replicated, may hold values from -7 to -2.5
- a_log: float32 [32], replicated, may hold values from -1.5 to 2.7
- d_skip: float32 [32], replicated, may hold values from 0.5 to 1.5
- norm_gain: float32 [2048], replicated, may hold values from 0.5 to 1.5
- pre_gain: float32 [1024], replicated, may hold values from 0.5 to 1.5
Outputs:
- output: float32 [16384, 1024], P(('dp', 'tensor'))
- grad_residual: float32 [16384, 1024], P(('dp', 'tensor'))
- grad_w_zx: float32 [1024, 2, 2048], P('dp', None, 'tensor')
- grad_w_bc: float32 [1024, 256], P('dp')
- grad_w_dt: float32 [1024, 32], P('dp', 'tensor')
- grad_w_out: float32 [2048, 1024], P('tensor', 'dp')
- grad_conv_weight: float32 [4, 2304], replicated
- grad_conv_bias: float32 [2304], replicated
- grad_dt_bias: float32 [32], replicated
- grad_a_log: float32 [32], replicated
- grad_d_skip: float32 [32], replicated
- grad_norm_gain: float32 [2048], replicated
- grad_pre_gain: float32 [1024], replicated
Inputs may be any that keep to these rules, and one draw needn't show every extreme that they name: `seq_ids`: each group of 2048 consecutive rows holds one or two whole sequences of 1024 to 2048 rows each, numbered 2 k and 2 k + 1 in group k, from the group's first row on, then rows marked -1; in every draw some group holds a single sequence of all its 2048 rows.
All inputs are finite; a program needn't handle non-finite values.
Results may differ from a plain program's by a relative error of at most 0.012.
The roundings to bfloat16 on the way count: a program that leaves them out, or rounds other values in their place, can miss the bound.
Values may be sent and summed in bfloat16 or wider, within the bound.
A program may use at most 128 MiB of HBM per device.

v0:
```python
import jax
import jax.numpy as jnp
from jax import lax
from jax.sharding import PartitionSpec as P

BLOCK = 256


EPSILON = 1e-05
HIGHEST = lax.Precision.HIGHEST
CONTRACT_ROWS = (((0,), (0,)), ((), ()))
CONTRACT_COLS = (((1,), (1,)), ((), ()))


def silu_of(value):
    return value * jax.nn.sigmoid(value)


def silu_slope(value):
    sigmoid_val = jax.nn.sigmoid(value)
    return sigmoid_val * (1.0 + value * (1.0 - sigmoid_val))


def rounded(value):
    return lax.optimization_barrier(value.astype(jnp.bfloat16)).astype(jnp.float32)


def matmul_rows(left_mat, right_mat):
    return lax.dot_general(left_mat, right_mat, CONTRACT_ROWS, preferred_element_type=jnp.float32)


def matmul_cols(left_mat, right_mat):
    return lax.dot_general(left_mat, right_mat, CONTRACT_COLS, preferred_element_type=jnp.float32)


def put_slice(total_vec, piece_vec, first_index, axis_pos):
    return lax.dynamic_update_slice_in_dim(total_vec, piece_vec, first_index, axis_pos)


def state_scan(
    inputs, b_rows, c_rows, raw_rates, bias_vec, log_rates, skip_gain, row_ids, previous, state_init
):
    row_count, head_count, head_dim = inputs.shape
    block_total = row_count // BLOCK
    step_size = jax.nn.softplus(raw_rates + bias_vec)
    log_decay = -jnp.exp(log_rates) * step_size
    lower_mask = jnp.arange(BLOCK)[:, None] >= jnp.arange(BLOCK)[None, :]

    def one_block(carry, block_data):
        state, last_id = carry
        block_in, block_b, block_c, block_dt, block_decay, block_ids = block_data
        cumulated = jnp.cumsum(block_decay, axis=0)
        together = (block_ids[:, None] == block_ids[None, :]) & lower_mask
        decay_gap = jnp.where(
            together[:, :, None], cumulated[:, None, :] - cumulated[None, :, :], 0.0
        )
        weights = jnp.where(together[:, :, None], jnp.exp(decay_gap), 0.0)
        scores = jnp.dot(block_c, block_b.T, precision=HIGHEST)
        mixing = scores[:, :, None] * weights * block_dt[None, :, :]
        inner_part = jnp.einsum("ijh,jhp->ihp", mixing, block_in, precision=HIGHEST)
        carried = jnp.where((block_ids == last_id)[:, None], jnp.exp(cumulated), 0.0)
        state_part = (
            jnp.einsum("in,hpn->ihp", block_c, state, precision=HIGHEST) * carried[:, :, None]
        )
        end_id = block_ids[-1]
        tail_weight = (
            jnp.where(
                (block_ids == end_id)[:, None], jnp.exp(cumulated[-1][None, :] - cumulated), 0.0
            )
            * block_dt
        )
        kept_share = jnp.where(end_id == last_id, jnp.exp(cumulated[-1]), 0.0)
        fresh_state = jnp.einsum(
            "jhp,jn->hpn", block_in * tail_weight[:, :, None], block_b, precision=HIGHEST
        )
        new_state = state * kept_share[:, None, None] + fresh_state
        block_out = inner_part + state_part + skip_gain[None, :, None] * block_in
        return ((new_state, end_id), block_out)

    block_data = (
        inputs.reshape(block_total, BLOCK, head_count, head_dim),
        b_rows.reshape(block_total, BLOCK, -1),
        c_rows.reshape(block_total, BLOCK, -1),
        step_size.reshape(block_total, BLOCK, head_count),
        log_decay.reshape(block_total, BLOCK, head_count),
        row_ids.reshape(block_total, BLOCK),
    )
    (final_state, _), outputs = lax.scan(
        jax.checkpoint(one_block), (state_init, previous), block_data
    )
    return (outputs.reshape(row_count, head_count, head_dim), final_state, log_decay)


def conv_apply(conv_in, weight, bias_vec, row_ids, rim_rows, rim_ids):
    row_count = conv_in.shape[0]
    margin = rim_rows.shape[0]
    extended = jnp.concatenate([rim_rows, conv_in], axis=0)
    extended_ids = jnp.concatenate([rim_ids, row_ids])
    pre_act = bias_vec + weight[0] * conv_in
    for offset in range(1, weight.shape[0]):
        shifted = extended[margin - offset : margin - offset + row_count]
        joined = extended_ids[margin - offset : margin - offset + row_count] == row_ids
        pre_act = pre_act + weight[offset] * shifted * joined[:, None]
    return silu_of(pre_act)


def local(
    residual,
    cotangent,
    seq_ids,
    w_zx,
    w_bc,
    w_dt,
    w_out,
    conv_weight,
    conv_bias,
    dt_bias,
    a_log,
    d_skip,
    norm_gain,
    pre_gain,
):
    tensor_index = lax.axis_index("tensor")
    own_rows = residual.shape[0]
    group_rows = seq_ids.shape[0]
    model_width = residual.shape[1]
    state_width = w_bc.shape[1] // 2
    heads_all = dt_bias.shape[0]
    inner_all = norm_gain.shape[0]
    head_dim = inner_all // heads_all
    margin = conv_weight.shape[0] - 1
    channels_all = conv_weight.shape[1]
    residual_f = residual.astype(jnp.float32)
    inv_rms = lax.rsqrt(jnp.mean(residual_f * residual_f, axis=1, keepdims=True) + EPSILON)
    normed = (residual_f * inv_rms * pre_gain).astype(jnp.bfloat16)
    zx_w, bc_w, dt_w, out_w = (
        lax.all_gather(w_zx, "dp", axis=0, tiled=True),
        lax.all_gather(w_bc, "dp", axis=0, tiled=True),
        lax.all_gather(w_dt, "dp", axis=0, tiled=True),
        lax.all_gather(w_out, "dp", axis=1, tiled=True),
    )
    own_ids = lax.dynamic_slice_in_dim(seq_ids, tensor_index * own_rows, own_rows)
    live_rows = (own_ids >= 0).astype(jnp.float32)[:, None]
    grad_cot = cotangent * live_rows.astype(jnp.bfloat16)
    heads_here = dt_w.shape[1]
    inner_here = heads_here * head_dim
    col_start = tensor_index * inner_here
    head_start = tensor_index * heads_here
    rows_normed = lax.all_gather(normed, "tensor", axis=0, tiled=True)
    w_head = jnp.concatenate([zx_w.reshape(model_width, 2 * inner_here), dt_w], axis=1)
    w_local = jnp.concatenate([zx_w.reshape(model_width, 2 * inner_here), bc_w, dt_w], axis=1)
    projected = jnp.dot(rows_normed, w_local, preferred_element_type=jnp.float32).astype(
        jnp.bfloat16
    )
    gate_in = projected[:, :inner_here].astype(jnp.float32)
    conv_in = projected[:, inner_here : 2 * inner_here + 2 * state_width]
    raw_rates = projected[:, 2 * inner_here + 2 * state_width :]
    conv_w_here = jnp.concatenate(
        [
            lax.dynamic_slice_in_dim(conv_weight, col_start, inner_here, 1),
            conv_weight[:, inner_all:],
        ],
        axis=1,
    )
    conv_b_here = jnp.concatenate(
        [lax.dynamic_slice_in_dim(conv_bias, col_start, inner_here), conv_bias[inner_all:]]
    )
    dt_b_here = lax.dynamic_slice_in_dim(dt_bias, head_start, heads_here)
    logs_here = lax.dynamic_slice_in_dim(a_log, head_start, heads_here)
    skip_here = lax.dynamic_slice_in_dim(d_skip, head_start, heads_here)
    gain_here = lax.dynamic_slice_in_dim(norm_gain, col_start, inner_here)
    rim_rows = jnp.zeros((margin, conv_in.shape[1]), jnp.float32)
    rim_ids = jnp.full((margin,), -2, jnp.int32)

    def conv_local(values, weight, bias_vec):
        return conv_apply(values, weight, bias_vec, seq_ids, rim_rows, rim_ids)

    activated, conv_pull = jax.vjp(
        conv_local, conv_in.astype(jnp.float32), conv_w_here, conv_b_here
    )
    inputs = rounded(activated[:, :inner_here])
    b_rows = rounded(activated[:, inner_here : inner_here + state_width])
    c_rows = rounded(activated[:, inner_here + state_width :])
    state_init = jnp.zeros((heads_here, head_dim, state_width), jnp.float32)

    def scan_local(values, b_vals, c_vals, raw_vals, bias_vec, log_rates, skip_gain):
        mixed, final_state, log_decay = state_scan(
            values.reshape(group_rows, heads_here, head_dim),
            b_vals,
            c_vals,
            raw_vals,
            bias_vec,
            log_rates,
            skip_gain,
            seq_ids,
            jnp.int32(-2),
            state_init,
        )
        return (mixed.reshape(group_rows, inner_here), final_state, log_decay)

    (mixed, final_state, log_decay), scan_pull = jax.vjp(
        scan_local,
        inputs,
        b_rows,
        c_rows,
        raw_rates.astype(jnp.float32),
        dt_b_here,
        logs_here,
        skip_here,
    )
    mixed_f = rounded(mixed)
    gate_act = silu_of(gate_in)
    gated_rows = mixed_f * gate_act
    sum_sq = lax.psum(jnp.sum(gated_rows * gated_rows, axis=1), "tensor")
    row_scale = lax.rsqrt(sum_sq / inner_all + EPSILON)[:, None]
    branch = (gated_rows * row_scale * gain_here).astype(jnp.bfloat16)
    mix_rows = lax.psum_scatter(
        jnp.dot(branch, out_w, preferred_element_type=jnp.float32),
        "tensor",
        scatter_dimension=0,
        tiled=True,
    )
    output = residual_f + live_rows * mix_rows
    cot_rows = lax.all_gather(grad_cot, "tensor", axis=0, tiled=True)
    grad_out_w = matmul_rows(branch, cot_rows)
    grad_branch = matmul_cols(cot_rows, out_w)
    weighted = grad_branch * gain_here
    dots_total = lax.psum(jnp.sum(weighted * gated_rows, axis=1), "tensor")
    grad_gated = (
        row_scale * weighted - gated_rows * row_scale**3 * (dots_total / inner_all)[:, None]
    )
    gain_local = jnp.sum(grad_branch * gated_rows * row_scale, axis=0)
    grad_mixed = rounded(grad_gated * gate_act)
    grad_gate = (grad_gated * mixed_f * silu_slope(gate_in)).astype(jnp.bfloat16)
    grad_inputs, grad_b, grad_c, grad_raw, grad_dt_b, grad_logs, grad_skip = scan_pull(
        (grad_mixed, jnp.zeros_like(final_state), jnp.zeros_like(log_decay))
    )
    grad_conv_in, grad_conv_w, grad_conv_b = conv_pull(
        jnp.concatenate([grad_inputs, grad_b, grad_c], axis=1)
    )
    grad_bc = lax.psum(grad_conv_in[:, inner_here:], "tensor").astype(jnp.bfloat16)
    grad_head = jnp.concatenate(
        [
            grad_gate,
            grad_conv_in[:, :inner_here].astype(jnp.bfloat16),
            grad_raw.astype(jnp.bfloat16),
        ],
        axis=1,
    )
    grad_w_head = matmul_rows(rows_normed, grad_head)
    grad_bc_w = matmul_rows(rows_normed, grad_bc)
    own_bc = lax.dynamic_slice_in_dim(grad_bc, tensor_index * own_rows, own_rows)
    grad_normed = lax.psum_scatter(
        matmul_cols(grad_head, w_head), "tensor", scatter_dimension=0, tiled=True
    ) + matmul_cols(own_bc, bc_w)
    grad_zx_w = grad_w_head[:, : 2 * inner_here].reshape(model_width, 2, inner_here)
    grad_dt_w = grad_w_head[:, 2 * inner_here :]
    conv_w_full = jnp.zeros((margin + 1, channels_all), jnp.float32)
    conv_w_full = put_slice(conv_w_full, grad_conv_w[:, :inner_here], col_start, 1)
    conv_w_full = put_slice(conv_w_full, grad_conv_w[:, inner_here:], inner_all, 1)
    conv_b_full = jnp.zeros((channels_all,), jnp.float32)
    conv_b_full = put_slice(conv_b_full, grad_conv_b[:inner_here], col_start, 0)
    conv_b_full = put_slice(conv_b_full, grad_conv_b[inner_here:], inner_all, 0)
    dt_b_full = put_slice(jnp.zeros((heads_all,), jnp.float32), grad_dt_b, head_start, 0)
    logs_full = put_slice(jnp.zeros((heads_all,), jnp.float32), grad_logs, head_start, 0)
    skip_full = put_slice(jnp.zeros((heads_all,), jnp.float32), grad_skip, head_start, 0)
    gain_full = put_slice(jnp.zeros((inner_all,), jnp.float32), gain_local, col_start, 0)
    grad_pre = jnp.sum(grad_normed * residual_f * inv_rms, axis=0)
    grad_residual = (
        cotangent.astype(jnp.float32)
        + inv_rms * pre_gain * grad_normed
        - residual_f
        * inv_rms**3
        * jnp.mean(grad_normed * pre_gain * residual_f, axis=1, keepdims=True)
    )
    grad_zx_w, grad_bc_w, grad_dt_w, grad_out_w = (
        lax.psum_scatter(grad_zx_w, "dp", scatter_dimension=0, tiled=True),
        lax.psum_scatter(grad_bc_w, "dp", scatter_dimension=0, tiled=True),
        lax.psum_scatter(grad_dt_w, "dp", scatter_dimension=0, tiled=True),
        lax.psum_scatter(grad_out_w, "dp", scatter_dimension=1, tiled=True),
    )
    small_sums = lax.psum(
        (conv_w_full, conv_b_full, dt_b_full, logs_full, skip_full, gain_full, grad_pre),
        ("dp", "tensor"),
    )
    return (
        output,
        grad_residual,
        grad_zx_w,
        grad_bc_w,
        grad_dt_w,
        grad_out_w,
        small_sums[0],
        small_sums[1],
        small_sums[2],
        small_sums[3],
        small_sums[4],
        small_sums[5],
        small_sums[6],
    )


def solution(mesh):
    placed = (
        P(("dp", "tensor"), None),
        P(("dp", "tensor"), None),
        P("dp"),
        P("dp", None, "tensor"),
        P("dp", None),
        P("dp", "tensor"),
        P("tensor", "dp"),
        P(),
        P(),
        P(),
        P(),
        P(),
        P(),
        P(),
    )
    return jax.shard_map(
        local,
        mesh=mesh,
        in_specs=placed,
        out_specs=(
            P(("dp", "tensor"), None),
            P(("dp", "tensor"), None),
            P("dp", None, "tensor"),
            P("dp", None),
            P("dp", "tensor"),
            P("tensor", "dp"),
            P(),
            P(),
            P(),
            P(),
            P(),
            P(),
            P(),
        ),
        check_vma=False,
    )
```

profile of v0, /device:TPU:0, one launch (start us, length us, event | category | flops | bytes accessed | tf_op | source)
XLA Modules:
  0.0 1252.4 jit_solution(14280931147249443041)
XLA Ops:
  17.9 28.1 %all_gather.21 = bf16[1024,8]{0,1:T(8,128)(2,1)S(1)} all-gather(bf16[128,8]{0,1:T(8,128)(2,1)S(1)} %copy-done.53), channel_id=1, replica_groups=mesh['dp'=8,'tensor'=4] {'dp'}, dimensions={0}, use_global_device_ids=true | all-gather | bytes 18432 | tf_op jit(solution)/shard_map/all_gather | solution.py:139
  46.2 32.1 %all_gather.20 = bf16[1024,256]{1,0:T(8,128)(2,1)S(1)} all-gather(bf16[128,256]{1,0:T(8,128)(2,1)S(1)} %copy-done.28), channel_id=1, replica_groups=mesh['dp'=8,'tensor'=4] {'dp'}, dimensions={0}, use_global_device_ids=true | all-gather | bytes 589824 | tf_op jit(solution)/shard_map/all_gather | solution.py:138
  80.7 22.7 %all-gather.5.cloned.1.call-done = bf16[2048,1024]{1,0:T(8,128)(2,1)} async-done(((bf16[512,1024]{1,0:T(8,128)(2,1)}), bf16[2048,1024]{1,0:T(8,128)(2,1)}) %all-gather.5.cloned.1.call-update) | async-done | bytes 4194320 | tf_op jit(solution)/shard_map/all_gather | solution.py:149
  103.4 7.5 convolution_convert_fusion
  113.4 7.5 multiply_convert_fusion
  132.7 133.3 %while.48 = (s32[]{:T(128)}, f32[8,64,128]{2,1,0:T(8,128)S(1)}, s32[]{:T(128)}, bf16[8,256,8,64]{1,3,2,0:T(8,128)(2,1)S(1)}, f32[8,8,64,128]{3,2,1,0:T(8,128)}, ...) while((s32[]{:T(128)}, f32[8,64,128]{2,1,0:T(8,128)S(1)}, ...), condition=%wide.region_4.5_spmd.clone, body=%wide.region_1.4_spmd.clone.sunk | while | flops 910041600 | bytes 5777833 | solution.py:88
  141.3 3.6 fusion.224
  267.9 3.9 multiply_reduce_fusion.10
  271.9 6.0 psum.70
  278.0 9.1 multiply_reduce_fusion.8
  287.1 5.7 psum.71
  292.9 6.0 fusion.98
  299.4 3.9 copy.135
  309.0 378.1 %while.49 = (s32[]{:T(128)}, f32[8]{0:T(128)}, f32[8,64,128]{2,1,0:T(8,128)S(1)}, f32[8,256,8,64]{1,0,3,2:T(8,128)}, f32[8,256,128]{2,1,0:T(8,128)}, /*index=5*/...) while((s32[]{:T(128)}, f32[8]{0:T(128)}, ...), condition=%wide.region_24.25_spmd.clone, body=%wide.region_10.24_spmd.clone.sunk | while | flops 2127208960 | bytes 19449592 | solution.py:88
  325.0 4.1 fusion.247
  343.1 12.7 %dynamic_update_slice.133 = f32[8,256,8,64]{1,0,3,2:T(8,128)} dynamic-update-slice(f32[8,256,8,64]{1,0,3,2:T(8,128)} %get-tuple-element.1303, f32[1,256,8,64]{1,0,3,2:T(1,128)S(1)} %copy.145, s32[]{:T(128)S(6)} %sub.265, s32[]{:T(128)} %constant.145.clone.1..sunk.1, s32[]{:T(128)} %constant.145.clone.1..sunk.1, s32[]{:T(128)} %constant.145.clone.1..sunk.1) | dynamic-update-slice | bytes 1048580 | tf_op jit(solution)/shard_map/transpose(jvp())/while/body/jit(dynamic_update_index_in_dim)/dynamic_update_slice | solution.py:88
  371.6 4.1 fusion.247
  390.4 12.7 %dynamic_update_slice.133 = f32[8,256,8,64]{1,0,3,2:T(8,128)} dynamic-update-slice(f32[8,256,8,64]{1,0,3,2:T(8,128)} %get-tuple-element.1303, f32[1,256,8,64]{1,0,3,2:T(1,128)S(1)} %copy.145, s32[]{:T(128)S(6)} %sub.265, s32[]{:T(128)} %constant.145.clone.1..sunk.1, s32[]{:T(128)} %constant.145.clone.1..sunk.1, s32[]{:T(128)} %constant.145.clone.1..sunk.1) | dynamic-update-slice | bytes 1048580 | tf_op jit(solution)/shard_map/transpose(jvp())/while/body/jit(dynamic_update_index_in_dim)/dynamic_update_slice | solution.py:88
  418.9 4.1 fusion.247
  437.7 12.7 %dynamic_update_slice.133 = f32[8,256,8,64]{1,0,3,2:T(8,128)} dynamic-update-slice(f32[8,256,8,64]{1,0,3,2:T(8,128)} %get-tuple-element.1303, f32[1,256,8,64]{1,0,3,2:T(1,128)S(1)} %copy.145, s32[]{:T(128)S(6)} %sub.265, s32[]{:T(128)} %constant.145.clone.1..sunk.1, s32[]{:T(128)} %constant.145.clone.1..sunk.1, s32[]{:T(128)} %constant.145.clone.1..sunk.1) | dynamic-update-slice | bytes 1048580 | tf_op jit(solution)/shard_map/transpose(jvp())/while/body/jit(dynamic_update_index_in_dim)/dynamic_update_slice | solution.py:88
  466.2 4.1 fusion.247
  485.0 12.7 %dynamic_update_slice.133 = f32[8,256,8,64]{1,0,3,2:T(8,128)} dynamic-update-slice(f32[8,256,8,64]{1,0,3,2:T(8,128)} %get-tuple-element.1303, f32[1,256,8,64]{1,0,3,2:T(1,128)S(1)} %copy.145, s32[]{:T(128)S(6)} %sub.265, s32[]{:T(128)} %constant.145.clone.1..sunk.1, s32[]{:T(128)} %constant.145.clone.1..sunk.1, s32[]{:T(128)} %constant.145.clone.1..sunk.1) | dynamic-update-slice | bytes 1048580 | tf_op jit(solution)/shard_map/transpose(jvp())/while/body/jit(dynamic_update_index_in_dim)/dynamic_update_slice | solution.py:88
  513.5 4.1 fusion.247
  532.3 12.7 %dynamic_update_slice.133 = f32[8,256,8,64]{1,0,3,2:T(8,128)} dynamic-update-slice(f32[8,256,8,64]{1,0,3,2:T(8,128)} %get-tuple-element.1303, f32[1,256,8,64]{1,0,3,2:T(1,128)S(1)} %copy.145, s32[]{:T(128)S(6)} %sub.265, s32[]{:T(128)} %constant.145.clone.1..sunk.1, s32[]{:T(128)} %constant.145.clone.1..sunk.1, s32[]{:T(128)} %constant.145.clone.1..sunk.1) | dynamic-update-slice | bytes 1048580 | tf_op jit(solution)/shard_map/transpose(jvp())/while/body/jit(dynamic_update_index_in_dim)/dynamic_update_slice | solution.py:88
  560.8 4.1 fusion.247
  579.6 12.7 %dynamic_update_slice.133 = f32[8,256,8,64]{1,0,3,2:T(8,128)} dynamic-update-slice(f32[8,256,8,64]{1,0,3,2:T(8,128)} %get-tuple-element.1303, f32[1,256,8,64]{1,0,3,2:T(1,128)S(1)} %copy.145, s32[]{:T(128)S(6)} %sub.265, s32[]{:T(128)} %constant.145.clone.1..sunk.1, s32[]{:T(128)} %constant.145.clone.1..sunk.1, s32[]{:T(128)} %constant.145.clone.1..sunk.1) | dynamic-update-slice | bytes 1048580 | tf_op jit(solution)/shard_map/transpose(jvp())/while/body/jit(dynamic_update_index_in_dim)/dynamic_update_slice | solution.py:88
  608.1 4.1 fusion.247
  626.9 12.7 %dynamic_update_slice.133 = f32[8,256,8,64]{1,0,3,2:T(8,128)} dynamic-update-slice(f32[8,256,8,64]{1,0,3,2:T(8,128)} %get-tuple-element.1303, f32[1,256,8,64]{1,0,3,2:T(1,128)S(1)} %copy.145, s32[]{:T(128)S(6)} %sub.265, s32[]{:T(128)} %constant.145.clone.1..sunk.1, s32[]{:T(128)} %constant.145.clone.1..sunk.1, s32[]{:T(128)} %constant.145.clone.1..sunk.1) | dynamic-update-slice | bytes 1048580 | tf_op jit(solution)/shard_map/transpose(jvp())/while/body/jit(dynamic_update_index_in_dim)/dynamic_update_slice | solution.py:88
  655.4 4.1 fusion.247
  674.2 12.7 %dynamic_update_slice.133 = f32[8,256,8,64]{1,0,3,2:T(8,128)} dynamic-update-slice(f32[8,256,8,64]{1,0,3,2:T(8,128)} %get-tuple-element.1303, f32[1,256,8,64]{1,0,3,2:T(1,128)S(1)} %copy.145, s32[]{:T(128)S(6)} %sub.265, s32[]{:T(128)} %constant.145.clone.1..sunk.1, s32[]{:T(128)} %constant.145.clone.1..sunk.1, s32[]{:T(128)} %constant.145.clone.1..sunk.1) | dynamic-update-slice | bytes 1048580 | tf_op jit(solution)/shard_map/transpose(jvp())/while/body/jit(dynamic_update_index_in_dim)/dynamic_update_slice | solution.py:88
  690.4 4.3 copy.136
  694.8 14.4 %multiply_reduce_fusion.7 = (f32[768]{0:T(1024)S(1)}, f32[768]{0:T(1024)S(1)}, f32[768]{0:T(1024)S(1)}, f32[768]{0:T(1024)S(1)}, f32[768]{0:T(1024)S(1)}, /*index=5*/f32[2048,768]{0,1:T(8,128)S(1)}) fusion(f32[2048,768]{0,1:T(8,128)} %copy-done, f32[2048]{0:T(1024)S(1)} %copy-done.25, f32[2048]{0:T(1024)S(1)} %copy-done.27, f32[2048]{0:T(1024)S(1)} %copy-done.23, ...), kind=kLoop, calls=%fused_computation.153 | loop fusion | flops 37744896 | bytes 28351488 | tf_op jit(solution)/shard_map/transpose(jvp())/reduce_sum | solution.py:103
  712.8 9.1 fusion.96
  725.8 7.0 fusion.121
  736.1 7.2 copy.103
  744.9 9.4 fusion.109
  756.2 8.0 fusion.146
  768.8 42.6 %all-reduce.17 = bf16[2048,256]{0,1:T(8,128)(2,1)S(1)} all-reduce(f32[2048,256]{0,1:T(8,128)} %slice.220), channel_id=1, replica_groups=mesh['dp'=8,'tensor'=4] {'tensor'}, use_global_device_ids=true, to_apply=%region_26.27 | all-reduce | flops 524288 | bytes 3145728 | tf_op jit(solution)/shard_map/psum | solution.py:241
  811.5 4.8 fusion.154
  816.5 7.2 fusion.145
  826.9 74.4 %all-reduce.16.cloned.1.call-done = f32[1024,2,512]{2,1,0:T(2,128)} async-done(((f32[1024,2,512]{2,1,0:T(2,128)}), f32[1024,2,512]{2,1,0:T(2,128)}) %all-reduce.16.cloned.1.call-update) | async-done | bytes 4194320
  903.2 71.3 %reduce-scatter.8.cloned.1.call-done = f32[512,1024]{1,0:T(8,128)} async-done(((f32[2048,1024]{1,0:T(8,128)}), f32[512,1024]{1,0:T(8,128)}) %reduce-scatter.8.cloned.1.call-update) | async-done | bytes 2097168 | tf_op jit(solution)/shard_map/reduce_scatter | solution.py:253
  977.3 41.0 %all-reduce.12 = (f32[4,2304]{1,0:T(4,128)}, f32[2304]{0:T(1024)}, f32[32]{0:T(128)}, f32[32]{0:T(128)}, f32[32]{0:T(128)}, /*index=5*/f32[2048]{0:T(1024)}, f32[1024]{0:T(1024)}) all-reduce(f32[4,2304]{1,0:T(4,128)S(1)} %add_dynamic-update-slice_fusion, ...), channel_id=1, replica_groups=mesh['dp'=8,'tensor'=4] {'dp','tensor'}, use_global_device_ids=true, to_apply=%region_36.37 | all-reduce | flops 14688 | bytes 117504 | tf_op jit(solution)/shard_map/psum | solution.py:282
  1018.3 31.5 %reduce-scatter.6.cloned.1.call-done = f32[512,1024]{1,0:T(8,128)} async-done(((f32[2048,1024]{1,0:T(8,128)}), f32[512,1024]{1,0:T(8,128)}) %reduce-scatter.6.cloned.1.call-update) | async-done | bytes 2097168 | tf_op jit(solution)/shard_map/reduce_scatter | solution.py:217
  1049.7 4.8 fusion.117
  1054.5 52.5 %reduce-scatter.12.cloned.1.call-done = f32[128,8]{0,1:T(8,128)} async-done(((f32[1024,8]{0,1:T(8,128)}), f32[128,8]{0,1:T(8,128)}) %reduce-scatter.12.cloned.1.call-update) | async-done | bytes 4112 | tf_op jit(solution)/shard_map/reduce_scatter | solution.py:279
  1107.0 66.6 %reduce-scatter.10.cloned.1.call-done = f32[128,256]{1,0:T(8,128)} async-done(((f32[1024,256]{1,0:T(8,128)}), f32[128,256]{1,0:T(8,128)}) %reduce-scatter.10.cloned.1.call-update) | async-done | bytes 131088 | tf_op jit(solution)/shard_map/reduce_scatter | solution.py:278
  1173.6 71.7 %reduce-scatter.14.cloned.1.call-done = f32[512,128]{1,0:T(8,128)} async-done(((f32[512,1024]{1,0:T(8,128)}), f32[512,128]{1,0:T(8,128)}) %reduce-scatter.14.cloned.1.call-update) | async-done | bytes 262160 | tf_op jit(solution)/shard_map/reduce_scatter | solution.py:280
  (773 shorter events, 416.0 us)
Async XLA Ops:
  7.2 9.8 copy-start.55
  7.3 10.6 copy-start.53
  7.3 38.9 %copy-start.28 = (bf16[128,256]{1,0:T(8,128)(2,1)S(1)}, bf16[128,256]{1,0:T(8,128)(2,1)}, u32[]{:S(2)}) copy-start(bf16[128,256]{1,0:T(8,128)(2,1)} %param.22) | copy-start | bytes 196612
  7.3 71.2 %all-gather.7.cloned.1.call-start = ((), (), s32[]{:S(2)}) async-start(), calls=%async_computation.6 | async-start | bytes 2359296 | tf_op jit(solution)/shard_map/all_gather | solution.py:137
  8.0 70.3 %slice-start.3 = ((f32[2304]{0:T(1024)}), f32[256]{0:T(256)S(1)}, s32[]{:S(2)}) async-start(f32[2304]{0:T(1024)} %param.26), calls=%async_computation.18 | async-start | bytes 2048 | tf_op jit(solution)/shard_map/slice | solution.py:166
  8.0 70.3 %slice-start.2 = ((f32[4,2304]{1,0:T(4,128)}), f32[4,256]{1,0:T(4,128)S(1)}, s32[]{:S(2)}) async-start(f32[4,2304]{1,0:T(4,128)} %param.25), calls=%async_computation.17 | async-start | bytes 8192 | tf_op jit(solution)/shard_map/slice | solution.py:161
  8.0 95.3 %all-gather.5.cloned.1.call-start = ((), (), s32[]{:S(2)}) async-start(), calls=%async_computation.5 | async-start | bytes 5242880 | tf_op jit(solution)/shard_map/all_gather | solution.py:149
  10.1 68.3 %copy-start.41 = (f32[512]{0:T(512)}, f32[512]{0:T(512)S(1)}, u32[]{:S(2)}) copy-start(f32[512]{0:T(512)S(1)} %get-tuple-element.955) | copy-start | bytes 6148
  12.7 265.3 %all-gather.9.cloned.1.call-start = ((), (), s32[]{:S(2)}) async-start(), calls=%async_computation.7 | async-start | bytes 1179648 | tf_op jit(solution)/shard_map/all_gather | solution.py:140
  13.4 264.6 %all-gather.11.cloned.1.call-start = ((), (), s32[]{:S(2)}) async-start(), calls=%async_computation.9 | async-start | bytes 5242880 | tf_op jit(solution)/shard_map/all_gather | solution.py:224
  15.4 885.9 %all-reduce.16.cloned.1.call-start = ((), (), s32[]{:S(2)}) async-start(), calls=%async_computation.14 | async-start | bytes 8388608
  16.9 96.4 %copy-start.22 = (f32[2048]{0:T(1024)}, f32[2048]{0:T(1024)S(1)}, u32[]{:S(2)}) copy-start(f32[2048]{0:T(1024)S(1)} %get-tuple-element.951) | copy-start | bytes 24580
  16.9 96.5 %copy-start.24 = (f32[2048]{0:T(1024)}, f32[2048]{0:T(1024)S(1)}, u32[]{:S(2)}) copy-start(f32[2048]{0:T(1024)S(1)} %get-tuple-element.952) | copy-start | bytes 24580
  16.9 96.4 %copy-start.26 = (f32[2048]{0:T(1024)}, f32[2048]{0:T(1024)S(1)}, u32[]{:S(2)}) copy-start(f32[2048]{0:T(1024)S(1)} %get-tuple-element.953) | copy-start | bytes 24580
  17.0 114.1 %copy-start.49 = (f32[8]{0:T(128)}, f32[8]{0:T(128)S(1)}, u32[]{:S(2)}) copy-start(f32[8]{0:T(128)S(1)} %dynamic_slice.149) | copy-start | bytes 100
  17.1 114.0 %copy-start.51 = (f32[8]{0:T(128)}, f32[8]{0:T(128)S(1)}, u32[]{:S(2)}) copy-start(f32[8]{0:T(128)S(1)} %fusion.141) | copy-start | bytes 100
  17.9 275.0 %copy-start.44 = (f32[512]{0:T(512)}, f32[512]{0:T(512)S(1)}, u32[]{:S(2)}) copy-start(f32[512]{0:T(512)S(1)} %dynamic_slice.153) | copy-start | bytes 6148
  46.2 64.7 %copy-start.18 = (bf16[1024,8]{1,0:T(8,128)(2,1)}, bf16[1024,8]{1,0:T(8,128)(2,1)S(1)}, u32[]{:S(2)}) copy-start(bf16[1024,8]{1,0:T(8,128)(2,1)S(1)} %copy.90) | copy-start | bytes 49156
  78.3 32.6 %copy-start.12 = (bf16[1024,256]{1,0:T(8,128)(2,1)}, bf16[1024,256]{1,0:T(8,128)(2,1)S(1)}, u32[]{:S(2)}) copy-start(bf16[1024,256]{1,0:T(8,128)(2,1)S(1)} %all_gather.20) | copy-start | bytes 1572868
  78.4 35.0 %copy-start.31 = (f32[768]{0:T(1024)}, f32[768]{0:T(1024)S(1)}, u32[]{:S(2)}) copy-start(f32[768]{0:T(1024)S(1)} %get-tuple-element.836) | copy-start | bytes 9220
  78.4 35.0 %copy-start.33 = (f32[768]{0:T(1024)}, f32[768]{0:T(1024)S(1)}, u32[]{:S(2)}) copy-start(f32[768]{0:T(1024)S(1)} %get-tuple-element.837) | copy-start | bytes 9220
  78.4 35.0 %copy-start.35 = (f32[768]{0:T(1024)}, f32[768]{0:T(1024)S(1)}, u32[]{:S(2)}) copy-start(f32[768]{0:T(1024)S(1)} %get-tuple-element.838) | copy-start | bytes 9220
  78.4 35.0 %copy-start.37 = (f32[768]{0:T(1024)}, f32[768]{0:T(1024)S(1)}, u32[]{:S(2)}) copy-start(f32[768]{0:T(1024)S(1)} %get-tuple-element.839) | copy-start | bytes 9220
  80.7 30.2 %copy-start.7 = (bf16[128,8,2,512]{3,1,2,0:T(8,128)(2,1)}, bf16[128,8,2,512]{3,1,2,0:T(8,128)(2,1)S(1)}, u32[]{:S(2)}) copy-start(bf16[128,8,2,512]{3,1,2,0:T(8,128)(2,1)S(1)} %copy.132) | copy-start | bytes 6291460
  267.9 25.0 %copy-start.2 = (bf16[64,8,8,256]{3,1,2,0:T(8,128)(2,1)}, bf16[64,8,8,256]{3,1,2,0:T(8,128)(2,1)S(1)}, u32[]{:S(2)}) copy-start(bf16[64,8,8,256]{3,1,2,0:T(8,128)(2,1)S(1)} %copy.134) | copy-start | bytes 6291460
  277.9 15.0 %copy-start.39 = (f32[2048]{0:T(1024)}, f32[2048]{0:T(1024)S(1)}, u32[]{:S(2)}) copy-start(f32[2048]{0:T(1024)S(1)} %get-tuple-element.950) | copy-start | bytes 24580
  311.9 18.6 %copy-start.13 = (f32[256,8]{0,1:T(8,128)}, f32[256,8]{0,1:T(8,128)S(1)}, u32[]{:S(2)}) copy-start(f32[256,8]{0,1:T(8,128)S(1)} %get-tuple-element.1214) | copy-start | bytes 24580 | tf_op jit(solution)/shard_map/transpose(jvp())/while
  358.5 19.3 %copy-start.13 = (f32[256,8]{0,1:T(8,128)}, f32[256,8]{0,1:T(8,128)S(1)}, u32[]{:S(2)}) copy-start(f32[256,8]{0,1:T(8,128)S(1)} %get-tuple-element.1214) | copy-start | bytes 24580 | tf_op jit(solution)/shard_map/transpose(jvp())/while
  405.8 19.3 %copy-start.13 = (f32[256,8]{0,1:T(8,128)}, f32[256,8]{0,1:T(8,128)S(1)}, u32[]{:S(2)}) copy-start(f32[256,8]{0,1:T(8,128)S(1)} %get-tuple-element.1214) | copy-start | bytes 24580 | tf_op jit(solution)/shard_map/transpose(jvp())/while
  453.1 19.3 %copy-start.13 = (f32[256,8]{0,1:T(8,128)}, f32[256,8]{0,1:T(8,128)S(1)}, u32[]{:S(2)}) copy-start(f32[256,8]{0,1:T(8,128)S(1)} %get-tuple-element.1214) | copy-start | bytes 24580 | tf_op jit(solution)/shard_map/transpose(jvp())/while
  500.4 19.3 %copy-start.13 = (f32[256,8]{0,1:T(8,128)}, f32[256,8]{0,1:T(8,128)S(1)}, u32[]{:S(2)}) copy-start(f32[256,8]{0,1:T(8,128)S(1)} %get-tuple-element.1214) | copy-start | bytes 24580 | tf_op jit(solution)/shard_map/transpose(jvp())/while
  547.7 19.3 %copy-start.13 = (f32[256,8]{0,1:T(8,128)}, f32[256,8]{0,1:T(8,128)S(1)}, u32[]{:S(2)}) copy-start(f32[256,8]{0,1:T(8,128)S(1)} %get-tuple-element.1214) | copy-start | bytes 24580 | tf_op jit(solution)/shard_map/transpose(jvp())/while
  595.0 19.3 %copy-start.13 = (f32[256,8]{0,1:T(8,128)}, f32[256,8]{0,1:T(8,128)S(1)}, u32[]{:S(2)}) copy-start(f32[256,8]{0,1:T(8,128)S(1)} %get-tuple-element.1214) | copy-start | bytes 24580 | tf_op jit(solution)/shard_map/transpose(jvp())/while
  642.3 19.3 %copy-start.13 = (f32[256,8]{0,1:T(8,128)}, f32[256,8]{0,1:T(8,128)S(1)}, u32[]{:S(2)}) copy-start(f32[256,8]{0,1:T(8,128)S(1)} %get-tuple-element.1214) | copy-start | bytes 24580 | tf_op jit(solution)/shard_map/transpose(jvp())/while
  694.8 14.5 %copy-start.34 = (f32[768]{0:T(1024)S(1)}, f32[768]{0:T(1024)}, u32[]{:S(2)}) copy-start(f32[768]{0:T(1024)} %copy-done.33) | copy-start | bytes 9220
  694.8 14.5 %copy-start.36 = (f32[768]{0:T(1024)S(1)}, f32[768]{0:T(1024)}, u32[]{:S(2)}) copy-start(f32[768]{0:T(1024)} %copy-done.35) | copy-start | bytes 9220
  694.8 14.5 %copy-start.38 = (f32[768]{0:T(1024)S(1)}, f32[768]{0:T(1024)}, u32[]{:S(2)}) copy-start(f32[768]{0:T(1024)} %copy-done.37) | copy-start | bytes 9220
  743.3 231.2 %reduce-scatter.8.cloned.1.call-start = ((), (), s32[]{:S(2)}) async-start(), calls=%async_computation.10 | async-start | bytes 10485760 | tf_op jit(solution)/shard_map/reduce_scatter | solution.py:253
  754.4 295.4 %reduce-scatter.6.cloned.1.call-start = ((), (), s32[]{:S(2)}) async-start(), calls=%async_computation.8 | async-start | bytes 10485760 | tf_op jit(solution)/shard_map/reduce_scatter | solution.py:217
  764.3 342.8 %reduce-scatter.12.cloned.1.call-start = ((), (), s32[]{:S(2)}) async-start(), calls=%async_computation.12 | async-start | bytes 36864 | tf_op jit(solution)/shard_map/reduce_scatter | solution.py:279
  811.5 362.1 %reduce-scatter.10.cloned.1.call-start = ((), (), s32[]{:S(2)}) async-start(), calls=%async_computation.11 | async-start | bytes 1179648 | tf_op jit(solution)/shard_map/reduce_scatter | solution.py:278
  816.4 10.3 copy-start.56
  816.4 158.1 %copy-start.4 = (bf16[512,1024]{1,0:T(8,128)(2,1)S(1)}, bf16[512,1024]{1,0:T(8,128)(2,1)}, u32[]{:S(2)}) copy-start(bf16[512,1024]{1,0:T(8,128)(2,1)} %param.18) | copy-start | bytes 3145732
  816.4 158.1 %copy-start.30 = (f32[1024]{0:T(1024)S(1)}, f32[1024]{0:T(1024)}, u32[]{:S(2)}) copy-start(f32[1024]{0:T(1024)} %param.31) | copy-start | bytes 12292
  816.4 158.1 %copy-start.42 = (f32[512]{0:T(512)S(1)}, f32[512]{0:T(512)}, u32[]{:S(2)}) copy-start(f32[512]{0:T(512)} %copy-done.41) | copy-start | bytes 6148
  816.4 428.9 %reduce-scatter.14.cloned.1.call-start = ((), (), s32[]{:S(2)}) async-start(), calls=%async_computation.13 | async-start | bytes 2359296 | tf_op jit(solution)/shard_map/reduce_scatter | solution.py:280
  823.7 226.0 %copy-start.46 = (f32[512]{0:T(512)S(1)}, f32[512]{0:T(512)}, u32[]{:S(2)}) copy-start(f32[512]{0:T(512)} %get-tuple-element.954) | copy-start | bytes 6148
  823.7 226.0 %copy-start.47 = (f32[512]{0:T(512)S(1)}, f32[512]{0:T(512)}, u32[]{:S(2)}) copy-start(f32[512]{0:T(512)} %get-tuple-element.919) | copy-start | bytes 6148
  (55 other events, 352.3 us)
Sparse Core Ops, SparseCore 0:
  10.2 58.8 all-gather.6
  70.7 32.6 all-gather.4
  105.4 39.5 all-gather.8
  146.4 33.4 all-gather.10
  743.5 157.7 all-reduce.15
  903.7 70.7 reduce-scatter.7
  977.3 72.4 reduce-scatter.5
  1053.4 53.5 reduce-scatter.11
  1111.0 62.5 reduce-scatter.9
  1178.0 67.2 reduce-scatter.13
where the time goes:
time: 1280 us; the launch traced here: 1250 us
  waiting for transfers between devices  392 us (31%)
  local copies, waits for them, and re-layouts  275 us (21%)
  matrix products  229 us (18%)
  other arithmetic  161 us (13%)
  blocking collectives  156 us (12%)
  loops' own time  21.9 us (2%)
  between operations  16.1 us (1%)
    dynamic_update_slice x24, local copies, waits for them, and re-layouts, state_scan(): lax.scan(jax.checkpoint(one_block), (state_init, previous), block_data)  116 us
    dot_general x24, matrix products, one_block(): inner_part = jnp.einsum('ijh,jhp->ihp', mixing, block_in, precision=HIGHEST)  84 us
    unnamed x11, waiting for transfers between devices  75.9 us
    reduce_scatter x1, waiting for transfers between devices, local(): lax.psum_scatter(grad_out_w, 'dp', scatter_dimension=1, tiled=True)  71.7 us
    reduce_scatter x1, waiting for transfers between devices, local(): lax.psum_scatter(matmul_cols(grad_head, w_head), 'tensor', scatter_dimens...  71.3 us
    reduce_scatter x1, waiting for transfers between devices, local(): lax.psum_scatter(grad_bc_w, 'dp', scatter_dimension=0, tiled=True)  66.6 us
    reduce_scatter x1, waiting for transfers between devices, local(): lax.psum_scatter(grad_dt_w, 'dp', scatter_dimension=0, tiled=True)  52.5 us
    another operation x59, other arithmetic  48.3 us
  transfers between devices with their start and end apart: 10, of which 7 were waited for; matrix products, arithmetic and copies ran while one was open for 17% of the time, Pallas kernels for 0%

commit v1 on v0

v1 whole, which is shorter than its diff:
```python
import jax
import jax.numpy as jnp
from jax import lax
from jax.experimental import pallas as pl
from jax.experimental.pallas import tpu as pltpu
from jax.sharding import PartitionSpec as P

BLOCK = 256


EPSILON = 1e-05
HIGHEST = lax.Precision.HIGHEST
CONTRACT_ROWS = (((0,), (0,)), ((), ()))
CONTRACT_COLS = (((1,), (1,)), ((), ()))


def silu_of(value):
    return value * jax.nn.sigmoid(value)


def silu_slope(value):
    sigmoid_val = jax.nn.sigmoid(value)
    return sigmoid_val * (1.0 + value * (1.0 - sigmoid_val))


def rounded(value):
    return lax.optimization_barrier(value.astype(jnp.bfloat16)).astype(jnp.float32)


def matmul_rows(left_mat, right_mat):
    return lax.dot_general(left_mat, right_mat, CONTRACT_ROWS, preferred_element_type=jnp.float32)


def matmul_cols(left_mat, right_mat):
    return lax.dot_general(left_mat, right_mat, CONTRACT_COLS, preferred_element_type=jnp.float32)


def put_slice(total_vec, piece_vec, first_index, axis_pos):
    return lax.dynamic_update_slice_in_dim(total_vec, piece_vec, first_index, axis_pos)


def dot_of(left_mat, right_mat, left_dim, right_dim):
    return lax.dot_general(
        left_mat,
        right_mat,
        (((left_dim,), (right_dim,)), ((), ())),
        preferred_element_type=jnp.float32,
    )


def spread(cols, expand):
    return jnp.dot(cols, expand, precision=HIGHEST, preferred_element_type=jnp.float32)


def head_decay(cum_c, cum_r, mask, head):
    gap = jnp.where(mask, cum_c[:, head : head + 1] - cum_r[head : head + 1, :], -1e30)
    return jnp.exp(gap)


def block_mask(id_c, id_r):
    size = id_c.shape[0]
    row = lax.broadcasted_iota(jnp.int32, (size, size), 0)
    col = lax.broadcasted_iota(jnp.int32, (size, size), 1)
    return (row >= col) & (id_c == id_r)


def pair_masks(size, width, heads):
    lane = lax.broadcasted_iota(jnp.int32, (size, width), 1)
    part = width // heads
    return [(lane // part) == k for k in range(heads)]


def forward_kernel(
    x_ref, b_ref, c_ref, cumc_ref, cumr_ref, dtr_ref, ec_ref, tail_ref, kept_ref, skip_ref,
    idc_ref, idr_ref, expand_ref, y_ref, h_ref, state,
):
    heads = cumc_ref.shape[1]
    size, inner = x_ref.shape
    per = 128 * heads // inner

    @pl.when(pl.program_id(0) == 0)
    def _():
        state[...] = jnp.zeros_like(state)

    expand = expand_ref[...]
    x, b, c = x_ref[...], b_ref[...], c_ref[...]
    h_low = state[...].astype(jnp.bfloat16)
    h_ref[0] = h_low
    x_f = x.astype(jnp.float32)
    y_all = dot_of(c, h_low, 1, 0) * spread(ec_ref[...], expand) + skip_ref[...] * x_f
    scores = dot_of(c, b, 1, 1)
    mask = block_mask(idc_ref[...], idr_ref[...])
    cum_c, cum_r, dt_r = cumc_ref[...], cumr_ref[...], dtr_ref[...]
    sides = pair_masks(size, 128, per)
    for pair in range(heads // per):
        lanes = slice(128 * pair, 128 * pair + 128)
        x_pair = x[:, lanes]
        acc = y_all[:, lanes]
        for k in range(per):
            head = pair * per + k
            mix = scores * head_decay(cum_c, cum_r, mask, head) * dt_r[head : head + 1, :]
            part = jnp.where(sides[k], x_pair, jnp.zeros_like(x_pair))
            acc = acc + dot_of(mix.astype(jnp.bfloat16), part, 1, 0)
        y_ref[:, lanes] = acc.astype(y_ref.dtype)
    tail = spread(tail_ref[...], expand)
    state[...] = state[...] * kept_ref[0] + dot_of(b, (x_f * tail).astype(jnp.bfloat16), 0, 0)


def backward_kernel(
    x_ref, dy_ref, b_ref, c_ref, cumc_ref, cumr_ref, dtr_ref, ec_ref, tail_ref, rate_ref,
    kept_ref, skip_ref, idc_ref, idr_ref, expand_ref, h_ref,
    dx_ref, db_ref, dc_ref, row_ref, late_ref, col_ref, keep_ref, dskip_ref, grad,
):
    heads = cumc_ref.shape[1]
    size, inner = x_ref.shape
    per = 128 * heads // inner

    @pl.when(pl.program_id(0) == 0)
    def _():
        grad[...] = jnp.zeros_like(grad)

    expand = expand_ref[...]
    x, dy, b, c, h_low = x_ref[...], dy_ref[...], b_ref[...], c_ref[...], h_ref[0]
    x_f, dy_f = x.astype(jnp.float32), dy.astype(jnp.float32)
    g_now = grad[...]
    g_low = g_now.astype(jnp.bfloat16)
    early = spread(ec_ref[...], expand)
    tail = spread(tail_ref[...], expand)
    dy_early = dy_f * early
    dy_early_low = dy_early.astype(jnp.bfloat16)
    from_state = dot_of(c, h_low, 1, 0)
    to_state = dot_of(b, g_low, 1, 0)

    def by_head(value):
        return lax.dot_general(
            value, expand, CONTRACT_COLS, precision=HIGHEST, preferred_element_type=jnp.float32
        )

    late_ref[...] = by_head(x_f * to_state) * rate_ref[...]
    row_sums = by_head(dy_early * from_state)
    keep_ref[0] = jnp.sum(h_low.astype(jnp.float32) * g_now, axis=0, keepdims=True) * kept_ref[0]
    dskip_ref[0] = jnp.sum(x_f * dy_f, axis=0, keepdims=True)
    grad[...] = g_now * kept_ref[0] + dot_of(c, dy_early_low, 0, 0)
    dx_all = skip_ref[...] * dy_f + tail * to_state
    scores = dot_of(c, b, 1, 1)
    mask = block_mask(idc_ref[...], idr_ref[...])
    cum_c, cum_r, dt_r = cumc_ref[...], cumr_ref[...], dtr_ref[...]
    sides = pair_masks(size, 128, per)
    head_lane = lax.broadcasted_iota(jnp.int32, (size, heads), 1)
    d_scores = jnp.zeros((size, size), jnp.float32)
    for pair in range(heads // per):
        lanes = slice(128 * pair, 128 * pair + 128)
        x_pair, dy_pair = x[:, lanes], dy[:, lanes]
        acc = dx_all[:, lanes]
        for k in range(per):
            head = pair * per + k
            decay = head_decay(cum_c, cum_r, mask, head)
            dt_row = dt_r[head : head + 1, :]
            dy_part = jnp.where(sides[k], dy_pair, jnp.zeros_like(dy_pair))
            d_mix = dot_of(dy_part, x_pair, 1, 1) * decay
            d_scores = d_scores + d_mix * dt_row
            core = d_mix * scores
            col_ref[head : head + 1, :] = jnp.sum(core, axis=0, keepdims=True)
            row_sum = jnp.sum(core * dt_row, axis=1, keepdims=True)
            row_sums = row_sums + jnp.where(head_lane == head, row_sum, 0.0)
            mix = (scores * decay * dt_row).astype(jnp.bfloat16)
            acc = acc + dot_of(mix, dy_part, 0, 0)
        dx_ref[:, lanes] = acc
    row_ref[...] = row_sums
    d_low = d_scores.astype(jnp.bfloat16)
    dc_ref[...] = dot_of(d_low, b, 1, 0) + dot_of(dy_early_low, h_low, 1, 1)
    db_ref[...] = dot_of(d_low, c, 0, 0) + dot_of((x_f * tail).astype(jnp.bfloat16), g_low, 1, 1)


def scan_terms(raw_rates, bias_vec, log_rates, skip_gain, ids, inner):
    rows, heads = raw_rates.shape
    count = rows // BLOCK
    step = jax.nn.softplus(raw_rates + bias_vec)
    rate = -jnp.exp(log_rates)
    decay = rate * step
    lower = (jnp.arange(BLOCK)[:, None] >= jnp.arange(BLOCK)[None, :]).astype(jnp.float32)
    cum = jnp.einsum(
        "ij,bjh->bih", lower, decay.reshape(count, BLOCK, heads), precision=HIGHEST
    )
    blocks = ids.reshape(count, BLOCK)
    before = jnp.concatenate([jnp.full((1,), -2, ids.dtype), blocks[:-1, -1]])
    joins = (blocks == before[:, None])[:, :, None]
    stays = (blocks == blocks[:, -1:])[:, :, None]
    early = jnp.where(joins, jnp.exp(cum), 0.0)
    rest = jnp.where(stays, jnp.exp(cum[:, -1:] - cum), 0.0)
    tail = rest * step.reshape(count, BLOCK, heads)
    part = inner // heads
    kept = jnp.repeat(early[:, -1:], part, axis=2)
    expand = jnp.repeat(jnp.eye(heads, dtype=jnp.float32), part, axis=1)

    def flat(value):
        return value.reshape(rows, heads)

    return dict(
        step=step, decay=decay, rate=rate, lower=lower, count=count, kept=kept, expand=expand,
        cum=flat(cum), cum_r=flat(cum).T, step_r=step.T, early=flat(early), rest=flat(rest),
        tail=flat(tail), skip=jnp.repeat(skip_gain, part)[None, :],
        ids_c=ids[:, None], ids_r=ids[None, :],
    )


def scan_forward(x, b, c, t):
    rows, inner = x.shape
    width, heads = b.shape[1], t["cum"].shape[1]

    def tall(cols):
        return pl.BlockSpec((BLOCK, cols), lambda i: (i, 0))

    def wide(rows_):
        return pl.BlockSpec((rows_, BLOCK), lambda i: (0, i))

    def whole(shape):
        return pl.BlockSpec(shape, lambda i: (0, 0))

    per_block = pl.BlockSpec((1, 1, inner), lambda i: (i, 0, 0))
    return pl.pallas_call(
        forward_kernel,
        grid=(t["count"],),
        in_specs=[
            tall(inner), tall(width), tall(width), tall(heads), wide(heads), wide(heads),
            tall(heads), tall(heads), per_block, whole((1, inner)), tall(1), wide(1),
            whole((heads, inner)),
        ],
        out_specs=[tall(inner), pl.BlockSpec((1, width, inner), lambda i: (i, 0, 0))],
        out_shape=[
            jax.ShapeDtypeStruct((rows, inner), jnp.bfloat16),
            jax.ShapeDtypeStruct((t["count"], width, inner), jnp.bfloat16),
        ],
        scratch_shapes=[pltpu.VMEM((width, inner), jnp.float32)],
        compiler_params=pltpu.CompilerParams(vmem_limit_bytes=40 * 2**20),
        cost_estimate=pl.CostEstimate(
            flops=4 * 10**9, bytes_accessed=8 * 2**20, transcendentals=4 * 2**20
        ),
        name="scan_forward",
    )(
        x, b, c, t["cum"], t["cum_r"], t["step_r"], t["early"], t["tail"], t["kept"], t["skip"],
        t["ids_c"], t["ids_r"], t["expand"],
    )


def scan_backward(x, dy, b, c, states, t):
    rows, inner = x.shape
    width, heads = b.shape[1], t["cum"].shape[1]
    last = t["count"] - 1

    def tall(cols):
        return pl.BlockSpec((BLOCK, cols), lambda i: (last - i, 0))

    def wide(rows_):
        return pl.BlockSpec((rows_, BLOCK), lambda i: (0, last - i))

    def whole(shape):
        return pl.BlockSpec(shape, lambda i: (0, 0))

    per_block = pl.BlockSpec((1, 1, inner), lambda i: (last - i, 0, 0))
    f32 = jnp.float32
    dx, db, dc, row, late, col, keep, dskip = pl.pallas_call(
        backward_kernel,
        grid=(t["count"],),
        in_specs=[
            tall(inner), tall(inner), tall(width), tall(width), tall(heads), wide(heads),
            wide(heads), tall(heads), tall(heads), tall(heads), per_block, whole((1, inner)),
            tall(1), wide(1), whole((heads, inner)),
            pl.BlockSpec((1, width, inner), lambda i: (last - i, 0, 0)),
        ],
        out_specs=[
            tall(inner), tall(width), tall(width), tall(heads), tall(heads), wide(heads),
            per_block, per_block,
        ],
        out_shape=[
            jax.ShapeDtypeStruct((rows, inner), f32),
            jax.ShapeDtypeStruct((rows, width), f32),
            jax.ShapeDtypeStruct((rows, width), f32),
            jax.ShapeDtypeStruct((rows, heads), f32),
            jax.ShapeDtypeStruct((rows, heads), f32),
            jax.ShapeDtypeStruct((heads, rows), f32),
            jax.ShapeDtypeStruct((t["count"], 1, inner), f32),
            jax.ShapeDtypeStruct((t["count"], 1, inner), f32),
        ],
        scratch_shapes=[pltpu.VMEM((width, inner), f32)],
        compiler_params=pltpu.CompilerParams(vmem_limit_bytes=40 * 2**20),
        cost_estimate=pl.CostEstimate(
            flops=10 * 10**9, bytes_accessed=16 * 2**20, transcendentals=4 * 2**20
        ),
        name="scan_backward",
    )(
        x, dy, b, c, t["cum"], t["cum_r"], t["step_r"], t["early"], t["tail"], t["rest"],
        t["kept"], t["skip"], t["ids_c"], t["ids_r"], t["expand"], states,
    )
    count = t["count"]
    direct = col.T + late
    after = row - direct * t["step"]
    ends = jnp.sum((late * t["step"]).reshape(count, BLOCK, heads), axis=1)
    ends = ends + jnp.sum(keep.reshape(count, heads, -1), axis=2)
    d_decay = jnp.einsum(
        "ij,bih->bjh", t["lower"], after.reshape(count, BLOCK, heads), precision=HIGHEST
    )
    d_decay = (d_decay + ends[:, None, :]).reshape(rows, heads)
    d_step = direct + t["rate"] * d_decay
    d_logs = jnp.sum(d_decay * t["decay"], axis=0)
    d_skip = jnp.sum(dskip.reshape(count, heads, -1), axis=(0, 2))
    return dx, db, dc, d_step, d_logs, d_skip


def conv_apply(conv_in, weight, bias_vec, row_ids, rim_rows, rim_ids):
    row_count = conv_in.shape[0]
    margin = rim_rows.shape[0]
    extended = jnp.concatenate([rim_rows, conv_in], axis=0)
    extended_ids = jnp.concatenate([rim_ids, row_ids])
    pre_act = bias_vec + weight[0] * conv_in
    for offset in range(1, weight.shape[0]):
        shifted = extended[margin - offset : margin - offset + row_count]
        joined = extended_ids[margin - offset : margin - offset + row_count] == row_ids
        pre_act = pre_act + weight[offset] * shifted * joined[:, None]
    return silu_of(pre_act)


def local(
    residual,
    cotangent,
    seq_ids,
    w_zx,
    w_bc,
    w_dt,
    w_out,
    conv_weight,
    conv_bias,
    dt_bias,
    a_log,
    d_skip,
    norm_gain,
    pre_gain,
):
    tensor_index = lax.axis_index("tensor")
    own_rows = residual.shape[0]
    group_rows = seq_ids.shape[0]
    model_width = residual.shape[1]
    state_width = w_bc.shape[1] // 2
    heads_all = dt_bias.shape[0]
    inner_all = norm_gain.shape[0]
    head_dim = inner_all // heads_all
    margin = conv_weight.shape[0] - 1
    channels_all = conv_weight.shape[1]
    residual_f = residual.astype(jnp.float32)
    inv_rms = lax.rsqrt(jnp.mean(residual_f * residual_f, axis=1, keepdims=True) + EPSILON)
    normed = (residual_f * inv_rms * pre_gain).astype(jnp.bfloat16)
    dt_cols, zx_cols = w_dt.shape[1], w_zx.shape[1] * w_zx.shape[2]
    w_part = jnp.concatenate([w_zx.reshape(w_zx.shape[0], zx_cols), w_bc, w_dt], axis=1)
    w_local = lax.all_gather(w_part, "dp", axis=0, tiled=True)
    out_wt = lax.all_gather(w_out.T, "dp", axis=0, tiled=True)
    bc_w = w_local[:, zx_cols : zx_cols + 2 * state_width]
    own_ids = lax.dynamic_slice_in_dim(seq_ids, tensor_index * own_rows, own_rows)
    live_rows = (own_ids >= 0).astype(jnp.float32)[:, None]
    grad_cot = cotangent * live_rows.astype(jnp.bfloat16)
    heads_here = dt_cols
    inner_here = heads_here * head_dim
    col_start = tensor_index * inner_here
    head_start = tensor_index * heads_here
    rows_normed = lax.all_gather(normed, "tensor", axis=0, tiled=True)
    projected = jnp.dot(rows_normed, w_local, preferred_element_type=jnp.float32).astype(
        jnp.bfloat16
    )
    gate_in = projected[:, :inner_here].astype(jnp.float32)
    conv_in = projected[:, inner_here : 2 * inner_here + 2 * state_width]
    raw_rates = projected[:, 2 * inner_here + 2 * state_width :]
    conv_w_here = jnp.concatenate(
        [
            lax.dynamic_slice_in_dim(conv_weight, col_start, inner_here, 1),
            conv_weight[:, inner_all:],
        ],
        axis=1,
    )
    conv_b_here = jnp.concatenate(
        [lax.dynamic_slice_in_dim(conv_bias, col_start, inner_here), conv_bias[inner_all:]]
    )
    dt_b_here = lax.dynamic_slice_in_dim(dt_bias, head_start, heads_here)
    logs_here = lax.dynamic_slice_in_dim(a_log, head_start, heads_here)
    skip_here = lax.dynamic_slice_in_dim(d_skip, head_start, heads_here)
    gain_here = lax.dynamic_slice_in_dim(norm_gain, col_start, inner_here)
    rim_rows = jnp.zeros((margin, conv_in.shape[1]), jnp.float32)
    rim_ids = jnp.full((margin,), -2, jnp.int32)

    def conv_local(values, weight, bias_vec):
        return conv_apply(values, weight, bias_vec, seq_ids, rim_rows, rim_ids)

    activated, conv_pull = jax.vjp(
        conv_local, conv_in.astype(jnp.float32), conv_w_here, conv_b_here
    )
    activated = lax.optimization_barrier(activated.astype(jnp.bfloat16))
    inputs = activated[:, :inner_here]
    b_rows = activated[:, inner_here : inner_here + state_width]
    c_rows = activated[:, inner_here + state_width :]
    raw_f = raw_rates.astype(jnp.float32)
    terms = scan_terms(raw_f, dt_b_here, logs_here, skip_here, seq_ids, inner_here)
    mixed, states = scan_forward(inputs, b_rows, c_rows, terms)
    mixed_f = mixed.astype(jnp.float32)
    gate_act = silu_of(gate_in)
    gated_rows = mixed_f * gate_act
    sum_sq = lax.psum(jnp.sum(gated_rows * gated_rows, axis=1), "tensor")
    row_scale = lax.rsqrt(sum_sq / inner_all + EPSILON)[:, None]
    branch = (gated_rows * row_scale * gain_here).astype(jnp.bfloat16)
    mix_rows = lax.psum_scatter(
        matmul_cols(branch, out_wt).astype(jnp.bfloat16),
        "tensor",
        scatter_dimension=0,
        tiled=True,
    ).astype(jnp.float32)
    output = residual_f + live_rows * mix_rows
    cot_rows = lax.all_gather(grad_cot, "tensor", axis=0, tiled=True)
    grad_out_w = matmul_rows(cot_rows, branch).astype(jnp.bfloat16)
    grad_out_w = lax.psum_scatter(grad_out_w, "dp", scatter_dimension=0, tiled=True)
    grad_branch = jnp.dot(cot_rows, out_wt, preferred_element_type=jnp.float32)
    weighted = grad_branch * gain_here
    dots_total = lax.psum(jnp.sum(weighted * gated_rows, axis=1), "tensor")
    grad_gated = (
        row_scale * weighted - gated_rows * row_scale**3 * (dots_total / inner_all)[:, None]
    )
    gain_local = jnp.sum(grad_branch * gated_rows * row_scale, axis=0)
    grad_mixed = (grad_gated * gate_act).astype(jnp.bfloat16)
    grad_gate = (grad_gated * mixed_f * silu_slope(gate_in)).astype(jnp.bfloat16)
    grad_inputs, grad_b, grad_c, grad_step, grad_logs, grad_skip = scan_backward(
        inputs, grad_mixed, b_rows, c_rows, states, terms
    )
    grad_raw = grad_step * jax.nn.sigmoid(raw_f + dt_b_here)
    grad_dt_b = jnp.sum(grad_raw, axis=0)
    grad_conv_in, grad_conv_w, grad_conv_b = conv_pull(
        jnp.concatenate([grad_inputs, grad_b, grad_c], axis=1)
    )
    grad_bc = lax.psum(grad_conv_in[:, inner_here:].astype(jnp.bfloat16), "tensor")
    own_index = lax.broadcasted_iota(jnp.int32, (group_rows, 1), 0) // own_rows
    own_bc = jnp.where(own_index == tensor_index, grad_bc, jnp.zeros_like(grad_bc))
    grad_gate_in = jnp.concatenate([grad_gate, grad_conv_in[:, :inner_here].astype(jnp.bfloat16)], axis=1)
    grad_raw_low = grad_raw.astype(jnp.bfloat16)
    grad_all = jnp.concatenate([grad_gate_in, grad_bc, grad_raw_low], axis=1)
    grad_in_w = matmul_rows(rows_normed, grad_all).astype(jnp.bfloat16)
    grad_in_w = lax.psum_scatter(grad_in_w, "dp", scatter_dimension=0, tiled=True)
    grad_mine = jnp.concatenate([grad_gate_in, own_bc, grad_raw_low], axis=1)
    grad_normed = lax.psum_scatter(
        matmul_cols(grad_mine, w_local).astype(jnp.bfloat16),
        "tensor",
        scatter_dimension=0,
        tiled=True,
    ).astype(jnp.float32)
    conv_w_full = jnp.zeros((margin + 1, channels_all), jnp.float32)
    conv_w_full = put_slice(conv_w_full, grad_conv_w[:, :inner_here], col_start, 1)
    conv_w_full = put_slice(conv_w_full, grad_conv_w[:, inner_here:], inner_all, 1)
    conv_b_full = jnp.zeros((channels_all,), jnp.float32)
    conv_b_full = put_slice(conv_b_full, grad_conv_b[:inner_here], col_start, 0)
    conv_b_full = put_slice(conv_b_full, grad_conv_b[inner_here:], inner_all, 0)
    dt_b_full = put_slice(jnp.zeros((heads_all,), jnp.float32), grad_dt_b, head_start, 0)
    logs_full = put_slice(jnp.zeros((heads_all,), jnp.float32), grad_logs, head_start, 0)
    skip_full = put_slice(jnp.zeros((heads_all,), jnp.float32), grad_skip, head_start, 0)
    gain_full = put_slice(jnp.zeros((inner_all,), jnp.float32), gain_local, col_start, 0)
    grad_pre = jnp.sum(grad_normed * residual_f * inv_rms, axis=0)
    grad_residual = (
        cotangent.astype(jnp.float32)
        + inv_rms * pre_gain * grad_normed
        - residual_f
        * inv_rms**3
        * jnp.mean(grad_normed * pre_gain * residual_f, axis=1, keepdims=True)
    )
    grad_in_w = grad_in_w.astype(jnp.float32)
    grad_zx_w = grad_in_w[:, :zx_cols].reshape(w_zx.shape)
    grad_bc_w = grad_in_w[:, zx_cols : zx_cols + 2 * state_width]
    grad_dt_w = grad_in_w[:, zx_cols + 2 * state_width :]
    grad_out_w = grad_out_w.astype(jnp.float32).T
    small = [conv_w_full, conv_b_full, dt_b_full, logs_full, skip_full, gain_full, grad_pre]
    packed = lax.psum(jnp.concatenate([part.reshape(-1) for part in small]), ("dp", "tensor"))
    small_sums, first = [], 0
    for part in small:
        small_sums.append(packed[first : first + part.size].reshape(part.shape))
        first += part.size
    return (
        output,
        grad_residual,
        grad_zx_w,
        grad_bc_w,
        grad_dt_w,
        grad_out_w,
        small_sums[0],
        small_sums[1],
        small_sums[2],
        small_sums[3],
        small_sums[4],
        small_sums[5],
        small_sums[6],
    )


def solution(mesh):
    placed = (
        P(("dp", "tensor"), None),
        P(("dp", "tensor"), None),
        P("dp"),
        P("dp", None, "tensor"),
        P("dp", None),
        P("dp", "tensor"),
        P("tensor", "dp"),
        P(),
        P(),
        P(),
        P(),
        P(),
        P(),
        P(),
    )
    return jax.shard_map(
        local,
        mesh=mesh,
        in_specs=placed,
        out_specs=(
            P(("dp", "tensor"), None),
            P(("dp", "tensor"), None),
            P("dp", None, "tensor"),
            P("dp", None),
            P("dp", "tensor"),
            P("tensor", "dp"),
            P(),
            P(),
            P(),
            P(),
            P(),
            P(),
            P(),
        ),
        check_vma=False,
    )
```

time: 1280 us -> 583 us (0.46); the launches traced: 1250 us -> 573 us
  local copies, waits for them, and re-layouts: 275 us -> 80.9 us
  matrix products: 229 us -> 51.5 us
  waiting for transfers between devices: 392 us -> 260 us
  blocking collectives: 156 us -> 53.2 us
  other arithmetic: 161 us -> 68.5 us
  Pallas kernels: 0 us -> 42.8 us
  loops' own time: 21.9 us -> 0 us
    reduce_scatter x5 -> x3, waiting for transfers between devices: 294 us -> 75.7 us  [the longest x1 40.9 us: local(): lax.psum_scatter(matmul_cols(grad_mine, w_local).astype(jnp.bfloat16), 't...]
    dot_general x113 -> x3, matrix products: 182 us -> 9.75 us  [the longest x1 9.26 us: local(): grad_branch = jnp.dot(cot_rows, out_wt, preferred_element_type=jnp.float32)]
    dynamic_update_slice x24 -> x0, local copies, waits for them, and re-layouts: 116 us -> none  [state_scan(): lax.scan(jax.checkpoint(one_block), (state_init, previous), block_data)]
    all_gather x2 -> x0, blocking collectives: 60.2 us -> none  [the longest x1 32.1 us: local(): lax.all_gather(w_bc, 'dp', axis=0, tiled=True)]
    all_gather x2, waiting for transfers between devices: 0.04 us -> 51.8 us  [the longest x1 51.8 us: local(): w_local = lax.all_gather(w_part, 'dp', axis=0, tiled=True)]
    psum x2 -> x1, blocking collectives: 83.6 us -> 40.2 us  [local(): lax.psum(jnp.concatenate([part.reshape(-1) for part in small]), ('dp', 't...]
    pallas_call x0 -> x2, Pallas kernels: none -> 42.8 us  [the longest x1 28.5 us: scan_backward(): pl.pallas_call(backward_kernel, grid=(t['count'],), in_specs=[tall(inner)...]
    dynamic_slice x32 -> x0, local copies, waits for them, and re-layouts: 41.8 us -> none  [state_scan(): lax.scan(jax.checkpoint(one_block), (state_init, previous), block_data)]
  transfers between devices with their start and end apart: 10 -> 9, of which waited for: 7 -> 7; matrix products, arithmetic and copies ran while one was open for 17% -> 19% of each run, Pallas kernels for 0% -> 3%
where the time goes in v1:
time: 583 us; the launch traced here: 573 us
  waiting for transfers between devices  260 us (45%)
  local copies, waits for them, and re-layouts  80.9 us (14%)
  other arithmetic  68.5 us (12%)
  blocking collectives  53.2 us (9%)
  matrix products  51.5 us (9%)
  Pallas kernels  42.8 us (7%)
  between operations  14.8 us (3%)
    unnamed x10, waiting for transfers between devices  73.5 us
    all_gather x1, waiting for transfers between devices, local(): w_local = lax.all_gather(w_part, 'dp', axis=0, tiled=True)  51.8 us
    reduce_scatter x1, waiting for transfers between devices, local(): lax.psum_scatter(matmul_cols(grad_mine, w_local).astype(jnp.bfloat16), 't...  40.9 us
    psum x1, blocking collectives, local(): lax.psum(jnp.concatenate([part.reshape(-1) for part in small]), ('dp', 't...  40.2 us
    unnamed x89, local copies, waits for them, and re-layouts  36 us
    all_gather x1, waiting for transfers between devices, local(): rows_normed = lax.all_gather(normed, 'tensor', axis=0, tiled=True)  35.3 us
    reduce_scatter x1, waiting for transfers between devices, local(): lax.psum_scatter(grad_out_w, 'dp', scatter_dimension=0, tiled=True)  32.4 us
    pallas_call x1, Pallas kernels, scan_backward(): pl.pallas_call(backward_kernel, grid=(t['count'],), in_specs=[tall(inner)...  28.5 us
  transfers between devices with their start and end apart: 9, of which 7 were waited for; matrix products, arithmetic and copies ran while one was open for 19% of the time, Pallas kernels for 3%

profile of v1, /device:TPU:0, one launch (start us, length us, event | category | flops | bytes accessed | tf_op | source)
XLA Modules:
  0.0 572.8 jit_solution(18427449051273543258)
XLA Ops:
  9.2 1.6 pad_maximum_fusion.12
  10.9 1.5 fusion.21
  12.4 2.5 fusion.23
  19.5 51.8 %all-gather.7.cloned.1.call-done = bf16[1024,1288]{1,0:T(8,128)(2,1)} async-done(((bf16[128,1288]{1,0:T(8,128)(2,1)}), bf16[1024,1288]{1,0:T(8,128)(2,1)}) %all-gather.7.cloned.1.call-update) | async-done | bytes 2637840 | tf_op jit(solution)/shard_map/all_gather | solution.py:354
  71.3 35.3 %all-gather.5.cloned.1.call-done = bf16[2048,1024]{1,0:T(8,128)(2,1)} async-done(((bf16[512,1024]{1,0:T(8,128)(2,1)}), bf16[2048,1024]{1,0:T(8,128)(2,1)}) %all-gather.5.cloned.1.call-update) | async-done | bytes 4194320 | tf_op jit(solution)/shard_map/all_gather | solution.py:364
  106.6 8.4 %convolution_convert_fusion = bf16[2048,1288]{0,1:T(8,128)(2,1)S(1)} fusion(bf16[2048,1024]{1,0:T(8,128)(2,1)} %all-gather.5.cloned.1.call-done, bf16[1024,1288]{1,0:T(8,128)(2,1)} %all-gather.7.cloned.1.call-done), kind=kOutput, calls=%fused_computation.1 | convolution fusion | flops 5404901376 | bytes 12107776 | tf_op jit(solution)/shard_map/dot_general | solution.py:365
  115.1 2.2 copy-done.24
  117.8 1.4 copy.128
  119.5 1.3 copy.129
  120.8 1.3 copy.133.cumc_ref
  122.1 1.3 copy.136
  123.5 2.7 slice_convert_fusion
  126.2 7.5 %multiply_convert_fusion = (bf16[2048,768]{0,1:T(8,128)(2,1)S(1)}, f32[2048,768]{0,1:T(8,128)}) fusion(f32[2048]{0:T(1024)S(1)} %get-tuple-element.144, f32[768]{0:T(1024)S(1)} %get-tuple-element.109, f32[2048]{0:T(1024)S(1)} %get-tuple-element.145, f32[768]{0:T(1024)S(1)} %get-tuple-element.110, f32[2048]{0:T(1024)S(1)} %get-tuple-element.143, ...), kind=kLoop, calls=%fused_computation.18 | loop fusion | flops 25165824 | bytes 15768576 | tf_op jit(solution)/shard_map/convert_element_type | solution.py:394
  133.7 1.6 copy-done.29
  135.3 1.5 slice.172
  136.8 2.9 copy.130.x_ref
  139.6 2.3 fusion.60
  141.9 2.1 copy.132.c_ref
  144.0 2.0 copy.131.b_ref
  151.8 14.3 %scan_forward.1 = (bf16[2048,512]{1,0:T(8,128)(2,1)S(1)}, bf16[8,128,512]{2,1,0:T(8,128)(2,1)S(1)}) custom-call(bf16[2048,512]{1,0:T(8,128)(2,1)S(1)} %copy.130.x_ref, bf16[2048,128]{1,0:T(8,128)(2,1)S(1)} %copy-done.18, bf16[2048,128]{1,0:T(8,128)(2,1)S(1)} %copy-done.16, f32[2048,8]{1,0:T(8,128)S(1)} %copy-done.9, f32[8,2048]{1,0:T(8,128)S(1)} %bitcast.58, ...), custom_call_target="tpu_custom_call" | custom-call | flops 4000000000 | bytes 8388608 | tf_op jit(solution)/shard_map/scan_forward/pallas_call | solution.py:221
  168.5 3.9 copy.135
  172.4 3.8 multiply_reduce_fusion.6
  176.2 7.1 %psum.28 = f32[2048]{0:T(1024)S(1)} all-reduce(f32[2048]{0:T(1024)S(1)} %multiply_reduce_fusion.6), channel_id=1, replica_groups=mesh['dp'=8,'tensor'=4] {'tensor'}, use_global_device_ids=true, to_apply=%region_2.3 | all-reduce | flops 2048 | bytes 16384 | tf_op jit(solution)/shard_map/psum | solution.py:404
  183.4 9.3 %multiply_reduce_fusion.4 = (f32[512]{0:T(512)S(1)}, f32[2048]{0:T(1024)S(1)}, f32[2048,512]{0,1:T(8,128)}) fusion(f32[2048]{0:T(1024)S(1)} %get-tuple-element.140, bf16[2048,1288]{0,1:T(8,128)(2,1)} %copy-done.24, bf16[2048,512]{0,1:T(8,128)(2,1)} %copy.135, f32[512]{0:T(512)S(1)} %dynamic_slice.27, bf16[2048,1024]{1,0:T(8,128)(2,1)} %all-gather.11.cloned.1.call-done, ...), kind=kOutput, calls=%fused_computation.49 | convolution fusion | flops 2161112576 | bytes 13651968 | tf_op jit(solution)/shard_map/dot_general | solution.py:417
  192.7 5.9 %psum.29 = f32[2048]{0:T(1024)S(1)} all-reduce(f32[2048]{0:T(1024)S(1)} %get-tuple-element.102), channel_id=1, replica_groups=mesh['dp'=8,'tensor'=4] {'tensor'}, use_global_device_ids=true, to_apply=%region_5.6 | all-reduce | flops 2048 | bytes 16384 | tf_op jit(solution)/shard_map/psum | solution.py:419
  198.6 6.7 %fusion.11 = (bf16[2048,512]{0,1:T(8,128)(2,1)}, bf16[2048,512]{0,1:T(8,128)(2,1)}) fusion(bf16[2048,512]{0,1:T(8,128)(2,1)} %copy.135, f32[2048]{0:T(1024)S(1)} %broadcast_multiply_fusion.2, f32[2048]{0:T(1024)S(1)} %get-tuple-element.139, f32[2048,512]{0,1:T(8,128)} %get-tuple-element.148, f32[512]{0:T(512)S(1)} %dynamic_slice.27, ...), kind=kLoop, calls=%fused_computation.43 | loop fusion | flops 22020096 | bytes 12609536 | tf_op jit(solution)/shard_map/convert_element_type | solution.py:425
  205.3 3.9 copy.138.dy_ref
  217.5 28.5 %scan_backward.1 = (f32[2048,512]{1,0:T(8,128)}, f32[2048,128]{1,0:T(8,128)S(1)}, f32[2048,128]{1,0:T(8,128)S(1)}, f32[2048,8]{1,0:T(8,128)S(1)}, f32[2048,8]{1,...) custom-call(bf16[2048,512]{1,0:T(8,128)(2,1)S(1)} %copy.130.x_ref, ...), custom_call_target="tpu_custom_call" | custom-call | flops 10000000000 | bytes 16777216 | tf_op jit(solution)/shard_map/scan_backward/pallas_call | solution.py:262
  249.9 5.6 copy.143
  256.2 15.1 %multiply_reduce_fusion.3 = (f32[768]{0:T(1024)S(1)}, f32[768]{0:T(1024)S(1)}, f32[768]{0:T(1024)S(1)}, f32[768]{0:T(1024)S(1)}, f32[768]{0:T(1024)S(1)}, /*index=5*/f32[2048,768]{0,1:T(8,128)S(1)}) fusion(f32[2048,768]{0,1:T(8,128)} %copy-done.23, f32[2048]{0:T(1024)S(1)} %get-tuple-element.144, f32[2048]{0:T(1024)S(1)} %get-tuple-element.145, ...), kind=kLoop, calls=%fused_computation.14 | loop fusion | flops 37744896 | bytes 28351488 | tf_op jit(solution)/shard_map/transpose(jvp())/reduce_sum | solution.py:319
  271.2 5.6 multiply_multiply_fusion.2
  276.8 8.3 %fusion.3 = bf16[2048,768]{0,1:T(8,128)(2,1)S(1)} fusion(f32[2048,768]{0,1:T(8,128)} %get-tuple-element.123, f32[2048,768]{0,1:T(8,128)} %get-tuple-element.124, f32[2048,768]{0,1:T(8,128)S(1)} %get-tuple-element.122, f32[2048,768]{0,1:T(8,128)S(1)} %get-tuple-element.113, f32[768]{0:T(1024)S(1)} %get-tuple-element.107), kind=kLoop, calls=%fused_computation.8 | loop fusion | flops 7864320 | bytes 28314624 | tf_op jit(solution)/shard_map/convert.2
  285.2 1.7 copy-done.28
  288.0 6.7 %convolution_convert_fusion.2 = bf16[1024,512]{1,0:T(8,128)(2,1)} fusion(bf16[2048,1024]{1,0:T(8,128)(2,1)} %all-gather.11.cloned.1.call-done, f32[512]{0:T(512)S(1)} %dynamic_slice.27, f32[2048]{0:T(1024)S(1)} %get-tuple-element.140, bf16[2048,512]{0,1:T(8,128)(2,1)S(1)} %copy-done.25, bf16[2048,1288]{0,1:T(8,128)(2,1)} %copy-done.24), kind=kOutput, calls=%fused_computation.70 | convolution fusion | flops 2158493696 | bytes 9447424 | tf_op jit(solution)/shard_map/dot_general | solution.py:31
  294.7 3.4 slice.181
  301.4 23.9 %all-reduce.11.cloned.1.call-done = bf16[2048,256]{0,1:T(8,128)(2,1)} async-done(((bf16[2048,256]{0,1:T(8,128)(2,1)}), bf16[2048,256]{0,1:T(8,128)(2,1)}) %all-reduce.11.cloned.1.call-update) | async-done | bytes 1048592 | tf_op jit(solution)/shard_map/psum | solution.py:434
  325.3 9.4 %fusion.17 = bf16[1024,1288]{0,1:T(8,128)(2,1)S(1)} fusion(bf16[2048,1024]{1,0:T(8,128)(2,1)} %all-gather.5.cloned.1.call-done, bf16[2048,8]{0,1:T(8,128)(2,1)S(1)} %get-tuple-element.112, bf16[2048,256]{0,1:T(8,128)(2,1)} %all-reduce.11.cloned.1.call-done, bf16[2048,512]{0,1:T(8,128)(2,1)} %slice.181, bf16[2048,512]{0,1:T(8,128)(2,1)} %get-tuple-element.120), kind=kOutput, calls=%fused_computation.55 | convolution fusion | flops 5424685056 | bytes 12107776 | tf_op jit(solution)/shard_map/dot_general | solution.py:31
  334.7 2.9 copy.152
  337.7 1.4 broadcast_select_fusion
  339.5 10.4 %fusion.18 = bf16[2048,1024]{1,0:T(8,128)(2,1)} fusion(bf16[1024,1288]{1,0:T(8,128)(2,1)} %all-gather.7.cloned.1.call-done, bf16[2048,8]{0,1:T(8,128)(2,1)S(1)} %get-tuple-element.112, bf16[2048,256]{0,1:T(8,128)(2,1)S(1)} %broadcast_select_fusion, bf16[2048,512]{0,1:T(8,128)(2,1)S(1)} %copy-done.32, bf16[2048,512]{0,1:T(8,128)(2,1)} %get-tuple-element.120), kind=kOutput, calls=%fused_computation.56 | convolution fusion | flops 5425463296 | bytes 12107776 | tf_op jit(solution)/shard_map/dot_general | solution.py:35
  351.8 6.9 %convolution_convert_fusion.1 = bf16[2048,1024]{1,0:T(8,128)(2,1)} fusion(bf16[1024,512]{0,1:T(8,128)(2,1)S(1)} %copy-done.36, f32[512]{0:T(512)S(1)} %dynamic_slice.27, f32[2048]{0:T(1024)S(1)} %get-tuple-element.140, bf16[2048,512]{0,1:T(8,128)(2,1)S(1)} %copy-done.26, bf16[2048,1288]{0,1:T(8,128)(2,1)} %copy-done.24), kind=kOutput, calls=%fused_computation.57 | convolution fusion | flops 2160066560 | bytes 9447424 | tf_op jit(solution)/shard_map/dot_general | solution.py:35
  360.3 32.4 %reduce-scatter.11.cloned.1.call-done = bf16[128,512]{1,0:T(8,128)(2,1)} async-done(((bf16[1024,512]{1,0:T(8,128)(2,1)}), bf16[128,512]{1,0:T(8,128)(2,1)}) %reduce-scatter.11.cloned.1.call-update) | async-done | bytes 131088 | tf_op jit(solution)/shard_map/reduce_scatter | solution.py:416
  394.5 72.6 %reduce-scatter.13.cloned.1.call-done = bf16[128,1288]{1,0:T(8,128)(2,1)} async-done(((bf16[1024,1288]{1,0:T(8,128)(2,1)}), bf16[128,1288]{1,0:T(8,128)(2,1)}) %reduce-scatter.13.cloned.1.call-update) | async-done | bytes 329744
  472.5 40.9 %reduce-scatter.9.cloned.1.call-done = bf16[512,1024]{1,0:T(8,128)(2,1)} async-done(((bf16[2048,1024]{1,0:T(8,128)(2,1)}), bf16[512,1024]{1,0:T(8,128)(2,1)}) %reduce-scatter.9.cloned.1.call-update) | async-done | bytes 1048592 | tf_op jit(solution)/shard_map/reduce_scatter | solution.py:443
  513.4 2.1 fusion.27
  515.5 40.2 %psum.31 = f32[14688]{0:T(1024)S(1)} all-reduce(f32[14688]{0:T(1024)S(1)} %concatenate.42), channel_id=1, replica_groups=mesh['dp'=8,'tensor'=4] {'dp','tensor'}, use_global_device_ids=true, to_apply=%region_24.25 | all-reduce | flops 14688 | bytes 117504 | tf_op jit(solution)/shard_map/psum | solution.py:473
  558.9 2.4 reduce-scatter.7.cloned.1.call-done
  561.3 4.5 fusion.20
  (192 shorter events, 47.0 us)
Async XLA Ops:
  7.2 8.6 %copy-start.20 = (s32[2048]{0:T(1024)S(1)}, s32[2048]{0:T(1024)}, u32[]{:S(2)}) copy-start(s32[2048]{0:T(1024)} %param.16) | copy-start | bytes 24580
  7.2 8.6 %copy-start.30 = (bf16[512,1024]{1,0:T(8,128)(2,1)S(1)}, bf16[512,1024]{1,0:T(8,128)(2,1)}, u32[]{:S(2)}) copy-start(bf16[512,1024]{1,0:T(8,128)(2,1)} %param.15) | copy-start | bytes 3145732
  7.2 64.1 %all-gather.7.cloned.1.call-start = ((), (), s32[]{:S(2)}) async-start(), calls=%async_computation.5 | async-start | bytes 3244032 | tf_op jit(solution)/shard_map/all_gather | solution.py:354
  9.1 8.4 %copy-start.35 = (f32[2304]{0:T(1024)S(1)}, f32[2304]{0:T(1024)}, u32[]{:S(2)}) copy-start(f32[2304]{0:T(1024)} %param.22) | copy-start | bytes 27652
  9.1 8.4 %copy-start.34 = (f32[4,2304]{1,0:T(4,128)S(1)}, f32[4,2304]{1,0:T(4,128)}, u32[]{:S(2)}) copy-start(f32[4,2304]{1,0:T(4,128)} %param.21) | copy-start | bytes 110596
  9.1 8.5 %copy-start.37 = (f32[32]{0:T(128)S(1)}, f32[32]{0:T(128)}, u32[]{:S(2)}) copy-start(f32[32]{0:T(128)} %param.23) | copy-start | bytes 388
  9.2 8.6 %copy-start.38 = (f32[32]{0:T(128)S(1)}, f32[32]{0:T(128)}, u32[]{:S(2)}) copy-start(f32[32]{0:T(128)} %param.24) | copy-start | bytes 388
  9.2 8.6 %copy-start.39 = (f32[32]{0:T(128)S(1)}, f32[32]{0:T(128)}, u32[]{:S(2)}) copy-start(f32[32]{0:T(128)} %param.25) | copy-start | bytes 388
  10.8 8.5 %slice-start.1 = ((f32[2304]{0:T(1024)}), f32[256]{0:T(256)S(1)}, s32[]{:S(2)}) async-start(f32[2304]{0:T(1024)} %param.22), calls=%async_computation.14 | async-start | bytes 2048 | tf_op jit(solution)/shard_map/slice | solution.py:379
  10.8 8.7 %slice-start = ((f32[4,2304]{1,0:T(4,128)}), f32[4,256]{1,0:T(4,128)S(1)}, s32[]{:S(2)}) async-start(f32[4,2304]{1,0:T(4,128)} %param.21), calls=%async_computation.13 | async-start | bytes 8192 | tf_op jit(solution)/shard_map/slice | solution.py:374
  10.9 95.8 %all-gather.5.cloned.1.call-start = ((), (), s32[]{:S(2)}) async-start(), calls=%async_computation.4 | async-start | bytes 5242880 | tf_op jit(solution)/shard_map/all_gather | solution.py:364
  15.0 168.4 %all-gather.9.cloned.1.call-start = ((), (), s32[]{:S(2)}) async-start(), calls=%async_computation.6 | async-start | bytes 1179648 | tf_op jit(solution)/shard_map/all_gather | solution.py:355
  15.7 167.7 %all-gather.11.cloned.1.call-start = ((), (), s32[]{:S(2)}) async-start(), calls=%async_computation.8 | async-start | bytes 5242880 | tf_op jit(solution)/shard_map/all_gather | solution.py:414
  17.0 308.3 %all-reduce.11.cloned.1.call-start = ((), (), s32[]{:S(2)}) async-start(), calls=%async_computation.9 | async-start | bytes 2097152 | tf_op jit(solution)/shard_map/psum | solution.py:434
  115.0 2.3 copy-start.24
  126.2 7.5 %copy-start.23 = (f32[2048,768]{0,1:T(8,128)}, f32[2048,768]{0,1:T(8,128)S(1)}, u32[]{:S(2)}) copy-start(f32[2048,768]{0,1:T(8,128)S(1)} %slice_convert_fusion) | copy-start | bytes 18874372
  133.7 1.6 copy-start.29
  146.1 1.2 copy-start.1
  147.3 1.2 copy-start.5
  148.5 1.2 copy-start.9
  149.7 1.0 copy-start.16
  150.8 1.0 copy-start.18
  166.2 1.3 copy-start
  209.3 1.2 copy-start.2
  210.5 1.2 copy-start.6
  211.7 1.2 copy-start.10
  212.9 1.2 copy-start.11
  214.2 1.0 copy-start.17
  215.2 1.0 copy-start.19
  216.2 1.2 copy-start.22
  246.9 1.0 copy-start.7
  248.9 1.0 copy-start.14
  249.9 5.6 copy-start.15
  249.9 5.9 %copy-start.13 = (f32[2048,128]{1,0:T(8,128)S(1)}, f32[2048,128]{1,0:T(8,128)}, u32[]{:S(2)}) copy-start(f32[2048,128]{1,0:T(8,128)} %copy-done.12) | copy-start | bytes 3145732
  276.8 11.2 %copy-start.25 = (bf16[2048,512]{0,1:T(8,128)(2,1)S(1)}, bf16[2048,512]{0,1:T(8,128)(2,1)}, u32[]{:S(2)}) copy-start(bf16[2048,512]{0,1:T(8,128)(2,1)} %copy.135) | copy-start | bytes 6291460
  285.2 1.7 copy-start.28
  287.9 104.8 %reduce-scatter.11.cloned.1.call-start = ((), (), s32[]{:S(2)}) async-start(), calls=%async_computation.11 | async-start | bytes 1179648 | tf_op jit(solution)/shard_map/reduce_scatter | solution.py:416
  294.7 3.5 copy-start.8
  294.7 3.8 copy-start.4
  298.8 168.3 %reduce-scatter.13.cloned.1.call-start = ((), (), s32[]{:S(2)}) async-start(), calls=%async_computation.12 | async-start | bytes 3244032
  337.6 1.9 copy-start.32
  337.7 175.7 %reduce-scatter.9.cloned.1.call-start = ((), (), s32[]{:S(2)}) async-start(), calls=%async_computation.10 | async-start | bytes 5242880 | tf_op jit(solution)/shard_map/reduce_scatter | solution.py:443
  350.0 1.6 copy-start.26
  350.0 1.9 copy-start.36
  350.0 211.3 %reduce-scatter.7.cloned.1.call-start = ((), (), s32[]{:S(2)}) async-start(), calls=%async_computation.7 | async-start | bytes 5242880 | tf_op jit(solution)/shard_map/reduce_scatter | solution.py:407
  358.7 154.6 %copy-start.27 = (bf16[512,1024]{1,0:T(8,128)(2,1)S(1)}, bf16[512,1024]{1,0:T(8,128)(2,1)}, u32[]{:S(2)}) copy-start(bf16[512,1024]{1,0:T(8,128)(2,1)} %param.14) | copy-start | bytes 3145732
  358.7 154.6 %copy-start.33 = (f32[1024]{0:T(1024)S(1)}, f32[1024]{0:T(1024)}, u32[]{:S(2)}) copy-start(f32[1024]{0:T(1024)} %param.27) | copy-start | bytes 12292
  358.7 202.6 %copy-start.31 = (bf16[512,1024]{1,0:T(8,128)(2,1)S(1)}, bf16[512,1024]{1,0:T(8,128)(2,1)}, u32[]{:S(2)}) copy-start(bf16[512,1024]{1,0:T(8,128)(2,1)} %param.15) | copy-start | bytes 3145732
  (3 other events, 2.9 us)
Sparse Core Ops, SparseCore 0:
  10.9 60.3 all-gather.6
  73.5 33.0 all-gather.4
  108.7 39.5 all-gather.8
  149.7 33.5 all-gather.10
  288.1 37.2 all-reduce.10
  329.0 63.7 reduce-scatter.10
  396.3 70.8 reduce-scatter.12
  469.6 43.6 reduce-scatter.8
  516.0 45.2 reduce-scatter.6

commit v2 on v1

--- a/solution.py
+++ b/solution.py
@@ -71,19 +71,33 @@
 
 
 def forward_kernel(
-    x_ref, b_ref, c_ref, cumc_ref, cumr_ref, dtr_ref, ec_ref, tail_ref, kept_ref, skip_ref,
-    idc_ref, idr_ref, expand_ref, y_ref, h_ref, state,
+    u_ref, taps_ref, bias_ref, joins_ref, cumc_ref, cumr_ref, dtr_ref, ec_ref, tail_ref, kept_ref,
+    skip_ref, idc_ref, idr_ref, expand_ref, y_ref, h_ref, act_ref, state, ext,
 ):
     heads = cumc_ref.shape[1]
-    size, inner = x_ref.shape
+    size, inner = y_ref.shape
+    width = (u_ref.shape[1] - inner) // 2
     per = 128 * heads // inner
 
     @pl.when(pl.program_id(0) == 0)
     def _():
         state[...] = jnp.zeros_like(state)
+        ext[size : size + 8, :] = jnp.zeros((8, ext.shape[1]), jnp.float32)
 
     expand = expand_ref[...]
-    x, b, c = x_ref[...], b_ref[...], c_ref[...]
+    joins = joins_ref[...]
+    ext[0:8, :] = ext[size : size + 8, :]
+    ext[8 : size + 8, :] = u_ref[...].astype(jnp.float32)
+    for first in range(0, u_ref.shape[1], 128):
+        lanes = slice(first, first + 128)
+        pre = bias_ref[:, lanes] + taps_ref[0:1, lanes] * ext[8 : size + 8, lanes]
+        for k in range(1, taps_ref.shape[0]):
+            shifted = ext[8 - k : size + 8 - k, lanes] * joins[:, k - 1 : k]
+            pre = pre + taps_ref[k : k + 1, lanes] * shifted
+        act_ref[:, lanes] = silu_of(pre).astype(act_ref.dtype)
+    x = act_ref[:, :inner]
+    b = act_ref[:, inner : inner + width]
+    c = act_ref[:, inner + width :]
     h_low = state[...].astype(jnp.bfloat16)
     h_ref[0] = h_low
     x_f = x.astype(jnp.float32)
@@ -107,20 +121,31 @@
 
 
 def backward_kernel(
-    x_ref, dy_ref, b_ref, c_ref, cumc_ref, cumr_ref, dtr_ref, ec_ref, tail_ref, rate_ref,
+    act_ref, u_ref, past_ref, dy_ref, taps_ref, bias_ref, joins_ref, nexts_ref,
+    cumc_ref, cumr_ref, dtr_ref, ec_ref, tail_ref, rate_ref,
     kept_ref, skip_ref, idc_ref, idr_ref, expand_ref, h_ref,
-    dx_ref, db_ref, dc_ref, row_ref, late_ref, col_ref, keep_ref, dskip_ref, grad,
+    du_ref, conv_ref, row_ref, late_ref, col_ref, keep_ref, dskip_ref, grad, ext, past,
 ):
     heads = cumc_ref.shape[1]
-    size, inner = x_ref.shape
+    size, inner = dy_ref.shape
+    width = (u_ref.shape[1] - inner) // 2
+    tap_count = taps_ref.shape[0]
     per = 128 * heads // inner
 
     @pl.when(pl.program_id(0) == 0)
     def _():
         grad[...] = jnp.zeros_like(grad)
-
+        conv_ref[...] = jnp.zeros_like(conv_ref)
+        ext[0:8, :] = jnp.zeros((8, ext.shape[1]), jnp.float32)
+
+    ext[size : size + 8, :] = ext[0:8, :]
+    past[0:16, :] = past_ref[...].astype(jnp.float32)
+    past[16 : size + 16, :] = u_ref[...].astype(jnp.float32)
     expand = expand_ref[...]
-    x, dy, b, c, h_low = x_ref[...], dy_ref[...], b_ref[...], c_ref[...], h_ref[0]
+    dy, h_low = dy_ref[...], h_ref[0]
+    x = act_ref[:, :inner]
+    b = act_ref[:, inner : inner + width]
+    c = act_ref[:, inner + width :]
     x_f, dy_f = x.astype(jnp.float32), dy.astype(jnp.float32)
     g_now = grad[...]
     g_low = g_now.astype(jnp.bfloat16)
@@ -165,14 +190,34 @@
             row_sums = row_sums + jnp.where(head_lane == head, row_sum, 0.0)
             mix = (scores * decay * dt_row).astype(jnp.bfloat16)
             acc = acc + dot_of(mix, dy_part, 0, 0)
-        dx_ref[:, lanes] = acc
+        ext[0:size, lanes] = acc
     row_ref[...] = row_sums
     d_low = d_scores.astype(jnp.bfloat16)
-    dc_ref[...] = dot_of(d_low, b, 1, 0) + dot_of(dy_early_low, h_low, 1, 1)
-    db_ref[...] = dot_of(d_low, c, 0, 0) + dot_of((x_f * tail).astype(jnp.bfloat16), g_low, 1, 1)
-
-
-def scan_terms(raw_rates, bias_vec, log_rates, skip_gain, ids, inner):
+    x_tail = (x_f * tail).astype(jnp.bfloat16)
+    ext[0:size, inner : inner + width] = dot_of(d_low, c, 0, 0) + dot_of(x_tail, g_low, 1, 1)
+    ext[0:size, inner + width :] = dot_of(d_low, b, 1, 0) + dot_of(dy_early_low, h_low, 1, 1)
+    joins, nexts = joins_ref[...], nexts_ref[...]
+    for first in range(0, u_ref.shape[1], 128):
+        lanes = slice(first, first + 128)
+        moved = [past[16 : size + 16, lanes]]
+        for k in range(1, tap_count):
+            moved.append(past[16 - k : size + 16 - k, lanes] * joins[:, k - 1 : k])
+        pre = bias_ref[:, lanes]
+        for k in range(tap_count):
+            pre = pre + taps_ref[k : k + 1, lanes] * moved[k]
+        d_pre = ext[0:size, lanes] * silu_slope(pre)
+        ext[0:size, lanes] = d_pre
+        for k in range(tap_count):
+            conv_ref[k : k + 1, lanes] += jnp.sum(d_pre * moved[k], axis=0, keepdims=True)
+        conv_ref[tap_count : tap_count + 1, lanes] += jnp.sum(d_pre, axis=0, keepdims=True)
+        du = taps_ref[0:1, lanes] * d_pre
+        for k in range(1, tap_count):
+            later = ext[k : size + k, lanes] * nexts[:, k - 1 : k]
+            du = du + taps_ref[k : k + 1, lanes] * later
+        du_ref[:, lanes] = du.astype(du_ref.dtype)
+
+
+def scan_terms(raw_rates, bias_vec, log_rates, skip_gain, ids, inner, taps, conv_bias):
     rows, heads = raw_rates.shape
     count = rows // BLOCK
     step = jax.nn.softplus(raw_rates + bias_vec)
@@ -193,6 +238,12 @@
     kept = jnp.repeat(early[:, -1:], part, axis=2)
     expand = jnp.repeat(jnp.eye(heads, dtype=jnp.float32), part, axis=1)
 
+    joins, nexts = [], []
+    for k in range(1, taps.shape[0]):
+        same = (ids[k:] == ids[:-k]).astype(jnp.float32)
+        joins.append(jnp.pad(same, (k, 0)))
+        nexts.append(jnp.pad(same, (0, k)))
+
     def flat(value):
         return value.reshape(rows, heads)
 
@@ -200,13 +251,17 @@
         step=step, decay=decay, rate=rate, lower=lower, count=count, kept=kept, expand=expand,
         cum=flat(cum), cum_r=flat(cum).T, step_r=step.T, early=flat(early), rest=flat(rest),
         tail=flat(tail), skip=jnp.repeat(skip_gain, part)[None, :],
-        ids_c=ids[:, None], ids_r=ids[None, :],
-    )
-
-
-def scan_forward(x, b, c, t):
-    rows, inner = x.shape
-    width, heads = b.shape[1], t["cum"].shape[1]
+        ids_c=ids[:, None], ids_r=ids[None, :], joins=jnp.stack(joins, axis=1),
+        nexts=jnp.stack(nexts, axis=1), taps=taps, conv_bias=conv_bias[None, :],
+    )
+
+
+def scan_forward(u, t):
+    rows, heads = t["cum"].shape
+    inner = t["expand"].shape[1]
+    channels = t["taps"].shape[1]
+    width = (channels - inner) // 2
+    shifts = t["joins"].shape[1]
 
     def tall(cols):
         return pl.BlockSpec((BLOCK, cols), lambda i: (i, 0))
@@ -222,30 +277,41 @@
         forward_kernel,
         grid=(t["count"],),
         in_specs=[
-            tall(inner), tall(width), tall(width), tall(heads), wide(heads), wide(heads),
-            tall(heads), tall(heads), per_block, whole((1, inner)), tall(1), wide(1),
-            whole((heads, inner)),
-        ],
-        out_specs=[tall(inner), pl.BlockSpec((1, width, inner), lambda i: (i, 0, 0))],
+            tall(channels), whole(t["taps"].shape), whole((1, channels)), tall(shifts),
+            tall(heads), wide(heads), wide(heads), tall(heads), tall(heads), per_block,
+            whole((1, inner)), tall(1), wide(1), whole((heads, inner)),
+        ],
+        out_specs=[
+            tall(inner),
+            pl.BlockSpec((1, width, inner), lambda i: (i, 0, 0)),
+            tall(channels),
+        ],
         out_shape=[
             jax.ShapeDtypeStruct((rows, inner), jnp.bfloat16),
             jax.ShapeDtypeStruct((t["count"], width, inner), jnp.bfloat16),
-        ],
-        scratch_shapes=[pltpu.VMEM((width, inner), jnp.float32)],
+            jax.ShapeDtypeStruct((rows, channels), jnp.bfloat16),
+        ],
+        scratch_shapes=[
+            pltpu.VMEM((width, inner), jnp.float32),
+            pltpu.VMEM((BLOCK + 8, channels), jnp.float32),
+        ],
         compiler_params=pltpu.CompilerParams(vmem_limit_bytes=40 * 2**20),
         cost_estimate=pl.CostEstimate(
             flops=4 * 10**9, bytes_accessed=8 * 2**20, transcendentals=4 * 2**20
         ),
         name="scan_forward",
     )(
-        x, b, c, t["cum"], t["cum_r"], t["step_r"], t["early"], t["tail"], t["kept"], t["skip"],
-        t["ids_c"], t["ids_r"], t["expand"],
-    )
-
-
-def scan_backward(x, dy, b, c, states, t):
-    rows, inner = x.shape
-    width, heads = b.shape[1], t["cum"].shape[1]
+        u, t["taps"], t["conv_bias"], t["joins"], t["cum"], t["cum_r"], t["step_r"], t["early"],
+        t["tail"], t["kept"], t["skip"], t["ids_c"], t["ids_r"], t["expand"],
+    )
+
+
+def scan_backward(act, u, dy, states, t):
+    rows, heads = t["cum"].shape
+    inner = t["expand"].shape[1]
+    channels = t["taps"].shape[1]
+    width = (channels - inner) // 2
+    shifts = t["joins"].shape[1]
     last = t["count"] - 1
 
     def tall(cols):
@@ -259,37 +325,45 @@
 
     per_block = pl.BlockSpec((1, 1, inner), lambda i: (last - i, 0, 0))
     f32 = jnp.float32
-    dx, db, dc, row, late, col, keep, dskip = pl.pallas_call(
+    du, conv, row, late, col, keep, dskip = pl.pallas_call(
         backward_kernel,
         grid=(t["count"],),
         in_specs=[
-            tall(inner), tall(inner), tall(width), tall(width), tall(heads), wide(heads),
+            tall(channels), tall(channels),
+            pl.BlockSpec(
+                (16, channels), lambda i: (jnp.maximum((last - i) * (BLOCK // 16) - 1, 0), 0)
+            ),
+            tall(inner), whole(t["taps"].shape), whole((1, channels)), tall(shifts), tall(shifts),
+            tall(heads), wide(heads),
             wide(heads), tall(heads), tall(heads), tall(heads), per_block, whole((1, inner)),
             tall(1), wide(1), whole((heads, inner)),
             pl.BlockSpec((1, width, inner), lambda i: (last - i, 0, 0)),
         ],
         out_specs=[
-            tall(inner), tall(width), tall(width), tall(heads), tall(heads), wide(heads),
+            tall(channels), whole((8, channels)), tall(heads), tall(heads), wide(heads),
             per_block, per_block,
         ],
         out_shape=[
-            jax.ShapeDtypeStruct((rows, inner), f32),
-            jax.ShapeDtypeStruct((rows, width), f32),
-            jax.ShapeDtypeStruct((rows, width), f32),
+            jax.ShapeDtypeStruct((rows, channels), jnp.bfloat16),
+            jax.ShapeDtypeStruct((8, channels), f32),
             jax.ShapeDtypeStruct((rows, heads), f32),
             jax.ShapeDtypeStruct((rows, heads), f32),
             jax.ShapeDtypeStruct((heads, rows), f32),
             jax.ShapeDtypeStruct((t["count"], 1, inner), f32),
             jax.ShapeDtypeStruct((t["count"], 1, inner), f32),
         ],
-        scratch_shapes=[pltpu.VMEM((width, inner), f32)],
+        scratch_shapes=[
+            pltpu.VMEM((width, inner), f32),
+            pltpu.VMEM((BLOCK + 8, channels), f32),
+            pltpu.VMEM((BLOCK + 16, channels), f32),
+        ],
         compiler_params=pltpu.CompilerParams(vmem_limit_bytes=40 * 2**20),
         cost_estimate=pl.CostEstimate(
             flops=10 * 10**9, bytes_accessed=16 * 2**20, transcendentals=4 * 2**20
         ),
         name="scan_backward",
     )(
-        x, dy, b, c, t["cum"], t["cum_r"], t["step_r"], t["early"], t["tail"], t["rest"],
+        act, u, u, dy, t["taps"], t["conv_bias"], t["joins"], t["nexts"], t["cum"], t["cum_r"], t["step_r"], t["early"], t["tail"], t["rest"],
         t["kept"], t["skip"], t["ids_c"], t["ids_r"], t["expand"], states,
     )
     count = t["count"]
@@ -304,20 +378,53 @@
     d_step = direct + t["rate"] * d_decay
     d_logs = jnp.sum(d_decay * t["decay"], axis=0)
     d_skip = jnp.sum(dskip.reshape(count, heads, -1), axis=(0, 2))
-    return dx, db, dc, d_step, d_logs, d_skip
-
-
-def conv_apply(conv_in, weight, bias_vec, row_ids, rim_rows, rim_ids):
-    row_count = conv_in.shape[0]
-    margin = rim_rows.shape[0]
-    extended = jnp.concatenate([rim_rows, conv_in], axis=0)
-    extended_ids = jnp.concatenate([rim_ids, row_ids])
-    pre_act = bias_vec + weight[0] * conv_in
-    for offset in range(1, weight.shape[0]):
-        shifted = extended[margin - offset : margin - offset + row_count]
-        joined = extended_ids[margin - offset : margin - offset + row_count] == row_ids
-        pre_act = pre_act + weight[offset] * shifted * joined[:, None]
-    return silu_of(pre_act)
+    return du, conv, d_step, d_logs, d_skip
+
+
+def swap(value, axis, bit):
+    count = lax.axis_size(axis)
+    return lax.ppermute(value, axis, [(i, i ^ bit) for i in range(count)])
+
+
+def sum_all(value, axes):
+    for axis in axes:
+        bit = 1
+        while bit < lax.axis_size(axis):
+            value = value + swap(value, axis, bit)
+            bit *= 2
+    return value
+
+
+def gather_rows(block):
+    if lax.axis_size("tensor") != 4:
+        return lax.all_gather(block, "tensor", axis=0, tiled=True)
+    rows = block.shape[0]
+    index = lax.axis_index("tensor")
+    far = swap(block, "tensor", 2)
+    near = swap(block, "tensor", 1)
+    cross = swap(far, "tensor", 1)
+    total = jnp.zeros((4 * rows, block.shape[1]), block.dtype)
+    for bits, part in ((0, block), (1, near), (2, far), (3, cross)):
+        total = put_slice(total, part, (index ^ bits) * rows, 0)
+    return total
+
+
+def scatter_rows(total):
+    low = total.astype(jnp.bfloat16)
+    if lax.axis_size("tensor") != 4:
+        return lax.psum_scatter(low, "tensor", scatter_dimension=0, tiled=True).astype(jnp.float32)
+    rows, cols = total.shape[0] // 4, total.shape[1]
+    index = lax.axis_index("tensor")
+
+    def block_of(value, place):
+        return lax.dynamic_slice_in_dim(value, place * rows, rows, 0)
+
+    def chip_sum(place):
+        got = swap(block_of(low, place ^ 1), "tensor", 1)
+        return block_of(low, place).astype(jnp.float32) + got.astype(jnp.float32)
+
+    far = swap(chip_sum(index ^ 2).astype(jnp.bfloat16), "tensor", 2)
+    return chip_sum(index) + far.astype(jnp.float32)
 
 
 def local(
@@ -349,11 +456,13 @@
     residual_f = residual.astype(jnp.float32)
     inv_rms = lax.rsqrt(jnp.mean(residual_f * residual_f, axis=1, keepdims=True) + EPSILON)
     normed = (residual_f * inv_rms * pre_gain).astype(jnp.bfloat16)
-    dt_cols, zx_cols = w_dt.shape[1], w_zx.shape[1] * w_zx.shape[2]
-    w_part = jnp.concatenate([w_zx.reshape(w_zx.shape[0], zx_cols), w_bc, w_dt], axis=1)
-    w_local = lax.all_gather(w_part, "dp", axis=0, tiled=True)
-    out_wt = lax.all_gather(w_out.T, "dp", axis=0, tiled=True)
-    bc_w = w_local[:, zx_cols : zx_cols + 2 * state_width]
+    dt_cols = w_dt.shape[1]
+    w_in = lax.all_gather(
+        jnp.concatenate([w_zx[:, 1], w_bc, w_dt], axis=1), "dp", axis=0, tiled=True
+    )
+    w_rest = lax.all_gather(
+        jnp.concatenate([w_zx[:, 0], w_out.T], axis=1), "dp", axis=0, tiled=True
+    )
     own_ids = lax.dynamic_slice_in_dim(seq_ids, tensor_index * own_rows, own_rows)
     live_rows = (own_ids >= 0).astype(jnp.float32)[:, None]
     grad_cot = cotangent * live_rows.astype(jnp.bfloat16)
@@ -361,13 +470,11 @@
     inner_here = heads_here * head_dim
     col_start = tensor_index * inner_here
     head_start = tensor_index * heads_here
-    rows_normed = lax.all_gather(normed, "tensor", axis=0, tiled=True)
-    projected = jnp.dot(rows_normed, w_local, preferred_element_type=jnp.float32).astype(
-        jnp.bfloat16
-    )
-    gate_in = projected[:, :inner_here].astype(jnp.float32)
-    conv_in = projected[:, inner_here : 2 * inner_here + 2 * state_width]
-    raw_rates = projected[:, 2 * inner_here + 2 * state_width :]
+    rows_normed = gather_rows(normed)
+    cot_rows = gather_rows(grad_cot)
+    channels_here = inner_here + 2 * state_width
+    projected = jnp.dot(rows_normed, w_in, preferred_element_type=jnp.float32).astype(jnp.bfloat16)
+    raw_f = projected[:, channels_here:].astype(jnp.float32)
     conv_w_here = jnp.concatenate(
         [
             lax.dynamic_slice_in_dim(conv_weight, col_start, inner_here, 1),
@@ -382,70 +489,52 @@
     logs_here = lax.dynamic_slice_in_dim(a_log, head_start, heads_here)
     skip_here = lax.dynamic_slice_in_dim(d_skip, head_start, heads_here)
     gain_here = lax.dynamic_slice_in_dim(norm_gain, col_start, inner_here)
-    rim_rows = jnp.zeros((margin, conv_in.shape[1]), jnp.float32)
-    rim_ids = jnp.full((margin,), -2, jnp.int32)
-
-    def conv_local(values, weight, bias_vec):
-        return conv_apply(values, weight, bias_vec, seq_ids, rim_rows, rim_ids)
-
-    activated, conv_pull = jax.vjp(
-        conv_local, conv_in.astype(jnp.float32), conv_w_here, conv_b_here
-    )
-    activated = lax.optimization_barrier(activated.astype(jnp.bfloat16))
-    inputs = activated[:, :inner_here]
-    b_rows = activated[:, inner_here : inner_here + state_width]
-    c_rows = activated[:, inner_here + state_width :]
-    raw_f = raw_rates.astype(jnp.float32)
-    terms = scan_terms(raw_f, dt_b_here, logs_here, skip_here, seq_ids, inner_here)
-    mixed, states = scan_forward(inputs, b_rows, c_rows, terms)
+    terms = scan_terms(
+        raw_f, dt_b_here, logs_here, skip_here, seq_ids, inner_here, conv_w_here, conv_b_here
+    )
+    mixed, states, activated = scan_forward(projected, terms)
     mixed_f = mixed.astype(jnp.float32)
+    w_gate, out_wt = w_rest[:, :inner_here], w_rest[:, inner_here:]
+    gate_in = (
+        jnp.dot(rows_normed, w_gate, preferred_element_type=jnp.float32)
+        .astype(jnp.bfloat16)
+        .astype(jnp.float32)
+    )
+    grad_branch = jnp.dot(cot_rows, out_wt, preferred_element_type=jnp.float32)
+    weighted = grad_branch * gain_here
     gate_act = silu_of(gate_in)
     gated_rows = mixed_f * gate_act
-    sum_sq = lax.psum(jnp.sum(gated_rows * gated_rows, axis=1), "tensor")
+    row_sums = jnp.stack(
+        [jnp.sum(gated_rows * gated_rows, axis=1), jnp.sum(weighted * gated_rows, axis=1)]
+    )
+    sum_sq, dots_total = lax.psum(row_sums, "tensor")
     row_scale = lax.rsqrt(sum_sq / inner_all + EPSILON)[:, None]
     branch = (gated_rows * row_scale * gain_here).astype(jnp.bfloat16)
-    mix_rows = lax.psum_scatter(
-        matmul_cols(branch, out_wt).astype(jnp.bfloat16),
-        "tensor",
-        scatter_dimension=0,
-        tiled=True,
-    ).astype(jnp.float32)
-    output = residual_f + live_rows * mix_rows
-    cot_rows = lax.all_gather(grad_cot, "tensor", axis=0, tiled=True)
-    grad_out_w = matmul_rows(cot_rows, branch).astype(jnp.bfloat16)
-    grad_out_w = lax.psum_scatter(grad_out_w, "dp", scatter_dimension=0, tiled=True)
-    grad_branch = jnp.dot(cot_rows, out_wt, preferred_element_type=jnp.float32)
-    weighted = grad_branch * gain_here
-    dots_total = lax.psum(jnp.sum(weighted * gated_rows, axis=1), "tensor")
     grad_gated = (
         row_scale * weighted - gated_rows * row_scale**3 * (dots_total / inner_all)[:, None]
     )
     gain_local = jnp.sum(grad_branch * gated_rows * row_scale, axis=0)
     grad_mixed = (grad_gated * gate_act).astype(jnp.bfloat16)
     grad_gate = (grad_gated * mixed_f * silu_slope(gate_in)).astype(jnp.bfloat16)
-    grad_inputs, grad_b, grad_c, grad_step, grad_logs, grad_skip = scan_backward(
-        inputs, grad_mixed, b_rows, c_rows, states, terms
-    )
+    grad_rest = jnp.concatenate(
+        [matmul_rows(rows_normed, grad_gate), matmul_rows(cot_rows, branch)], axis=1
+    ).astype(jnp.bfloat16)
+    mix_part = matmul_cols(branch, out_wt).astype(jnp.bfloat16)
+    grad_mixed, grad_rest, mix_part = lax.optimization_barrier((grad_mixed, grad_rest, mix_part))
+    grad_rest = lax.psum_scatter(grad_rest, "dp", scatter_dimension=0, tiled=True)
+    output = residual_f + live_rows * scatter_rows(mix_part)
+    grad_conv_in, grad_conv, grad_step, grad_logs, grad_skip = scan_backward(
+        activated, projected, grad_mixed, states, terms
+    )
+    grad_conv_w, grad_conv_b = grad_conv[: margin + 1], grad_conv[margin + 1]
     grad_raw = grad_step * jax.nn.sigmoid(raw_f + dt_b_here)
     grad_dt_b = jnp.sum(grad_raw, axis=0)
-    grad_conv_in, grad_conv_w, grad_conv_b = conv_pull(
-        jnp.concatenate([grad_inputs, grad_b, grad_c], axis=1)
-    )
-    grad_bc = lax.psum(grad_conv_in[:, inner_here:].astype(jnp.bfloat16), "tensor")
-    own_index = lax.broadcasted_iota(jnp.int32, (group_rows, 1), 0) // own_rows
-    own_bc = jnp.where(own_index == tensor_index, grad_bc, jnp.zeros_like(grad_bc))
-    grad_gate_in = jnp.concatenate([grad_gate, grad_conv_in[:, :inner_here].astype(jnp.bfloat16)], axis=1)
-    grad_raw_low = grad_raw.astype(jnp.bfloat16)
-    grad_all = jnp.concatenate([grad_gate_in, grad_bc, grad_raw_low], axis=1)
-    grad_in_w = matmul_rows(rows_normed, grad_all).astype(jnp.bfloat16)
+    grad_in = jnp.concatenate([grad_conv_in, grad_raw.astype(jnp.bfloat16)], axis=1)
+    grad_in_w = matmul_rows(rows_normed, grad_in).astype(jnp.bfloat16)
     grad_in_w = lax.psum_scatter(grad_in_w, "dp", scatter_dimension=0, tiled=True)
-    grad_mine = jnp.concatenate([grad_gate_in, own_bc, grad_raw_low], axis=1)
-    grad_normed = lax.psum_scatter(
-        matmul_cols(grad_mine, w_local).astype(jnp.bfloat16),
-        "tensor",
-        scatter_dimension=0,
-        tiled=True,
-    ).astype(jnp.float32)
+    normed_part = matmul_cols(grad_gate, w_gate) + matmul_cols(grad_in, w_in)
+    grad_normed = scatter_rows(normed_part)
+    grad_pre = jnp.sum(normed_part * rows_normed.astype(jnp.float32), axis=0) / pre_gain
     conv_w_full = jnp.zeros((margin + 1, channels_all), jnp.float32)
     conv_w_full = put_slice(conv_w_full, grad_conv_w[:, :inner_here], col_start, 1)
     conv_w_full = put_slice(conv_w_full, grad_conv_w[:, inner_here:], inner_all, 1)
@@ -456,7 +545,6 @@
     logs_full = put_slice(jnp.zeros((heads_all,), jnp.float32), grad_logs, head_start, 0)
     skip_full = put_slice(jnp.zeros((heads_all,), jnp.float32), grad_skip, head_start, 0)
     gain_full = put_slice(jnp.zeros((inner_all,), jnp.float32), gain_local, col_start, 0)
-    grad_pre = jnp.sum(grad_normed * residual_f * inv_rms, axis=0)
     grad_residual = (
         cotangent.astype(jnp.float32)
         + inv_rms * pre_gain * grad_normed
@@ -465,12 +553,14 @@
         * jnp.mean(grad_normed * pre_gain * residual_f, axis=1, keepdims=True)
     )
     grad_in_w = grad_in_w.astype(jnp.float32)
-    grad_zx_w = grad_in_w[:, :zx_cols].reshape(w_zx.shape)
-    grad_bc_w = grad_in_w[:, zx_cols : zx_cols + 2 * state_width]
-    grad_dt_w = grad_in_w[:, zx_cols + 2 * state_width :]
-    grad_out_w = grad_out_w.astype(jnp.float32).T
+    grad_rest = grad_rest.astype(jnp.float32)
+    grad_zx_w = jnp.stack([grad_rest[:, :inner_here], grad_in_w[:, :inner_here]], axis=1)
+    grad_bc_w = sum_all(grad_in_w[:, inner_here:channels_here], ("tensor",))
+    grad_dt_w = grad_in_w[:, channels_here:]
+    grad_out_w = grad_rest[:, inner_here:].T
     small = [conv_w_full, conv_b_full, dt_b_full, logs_full, skip_full, gain_full, grad_pre]
-    packed = lax.psum(jnp.concatenate([part.reshape(-1) for part in small]), ("dp", "tensor"))
+    packed = jnp.concatenate([part.reshape(-1) for part in small])
+    packed = sum_all(packed, ("tensor", "dp"))
     small_sums, first = [], 0
     for part in small:
         small_sums.append(packed[first : first + part.size].reshape(part.shape))

time: 583 us -> 395 us (0.68)
  waiting for transfers between devices: 260 us -> 129 us
  blocking collectives: 53.2 us -> 12.1 us
  other arithmetic: 68.5 us -> 27.7 us
  Pallas kernels: 42.8 us -> 64.5 us
  local copies, waits for them, and re-layouts: 80.9 us -> 67.5 us
  starting transfers between devices: 0.83 us -> 13.8 us
  matrix products: 51.5 us -> 58 us
    ppermute x0 -> x19, waiting for transfers between devices: none -> 100 us  [swap(): return lax.ppermute(value, axis, [(i, i ^ bit) for i in range(count)])]
    all_gather x4 -> x2, waiting for transfers between devices: 87.1 us -> 0.01 us  [the longest x1 0.01 us: local(): lax.all_gather(jnp.concatenate([w_zx[:, 1], w_bc, w_dt], axis=1), 'dp', a...]
    reduce_scatter x3 -> x0, waiting for transfers between devices: 75.7 us -> none  [the longest x1 40.9 us: local(): lax.psum_scatter(matmul_cols(grad_mine, w_local).astype(jnp.bfloat16), 't...]
    unnamed x10 -> x6, waiting for transfers between devices: 73.5 us -> 28.5 us
    psum x3 -> x1, blocking collectives: 53.2 us -> 12.1 us  [local(): sum_sq, dots_total = lax.psum(row_sums, 'tensor')]
    psum x1 -> x0, waiting for transfers between devices: 23.9 us -> none  [local(): lax.psum(grad_conv_in[:, inner_here:].astype(jnp.bfloat16), 'tensor')]
    pallas_call x2, Pallas kernels: 42.8 us -> 64.5 us  [the longest x1 43.7 us: scan_backward(): pl.pallas_call(backward_kernel, grid=(t['count'],), in_specs=[tall(channe...]
    reduce_sum x3 -> x1, other arithmetic: 21 us -> 1.95 us  [local(): jnp.mean(grad_normed * pre_gain * residual_f, axis=1, keepdims=True)]
  transfers between devices with their start and end apart: 9 -> 23, of which waited for: 7 -> 10; matrix products, arithmetic and copies ran while one was open for 19% -> 22% of each run, Pallas kernels for 3% -> 5%
where the time goes in v2:
time: 395 us; the launch traced here: 387 us
  waiting for transfers between devices  129 us (33%)
  local copies, waits for them, and re-layouts  67.5 us (17%)
  Pallas kernels  64.5 us (16%)
  matrix products  58 us (15%)
  other arithmetic  27.7 us (7%)
  between operations  14.7 us (4%)
  starting transfers between devices  13.8 us (3%)
  blocking collectives  12.1 us (3%)
    ppermute x19, waiting for transfers between devices, swap(): return lax.ppermute(value, axis, [(i, i ^ bit) for i in range(count)])  100 us
    pallas_call x1, Pallas kernels, scan_backward(): pl.pallas_call(backward_kernel, grid=(t['count'],), in_specs=[tall(channe...  43.7 us
    unnamed x6, waiting for transfers between devices  28.5 us
    unnamed x79, local copies, waits for them, and re-layouts  23.2 us
    pallas_call x1, Pallas kernels, scan_forward(): pl.pallas_call(forward_kernel, grid=(t['count'],), in_specs=[tall(channel...  20.9 us
    dot_general x3, matrix products, matmul_rows(): lax.dot_general(left_mat, right_mat, CONTRACT_ROWS, preferred_element_typ...  19.2 us
    dot_general x3, matrix products, matmul_cols(): lax.dot_general(left_mat, right_mat, CONTRACT_COLS, preferred_element_typ...  16.7 us
    ppermute x19, starting transfers between devices, swap(): return lax.ppermute(value, axis, [(i, i ^ bit) for i in range(count)])  13.7 us
  transfers between devices with their start and end apart: 23, of which 10 were waited for; matrix products, arithmetic and copies ran while one was open for 22% of the time, Pallas kernels for 5%

profile of v2, /device:TPU:0, one launch (start us, length us, event | category | flops | bytes accessed | tf_op | source)
XLA Modules:
  0.0 387.3 jit_solution(1147668724213739789)
XLA Ops:
  8.1 1.5 fusion.41
  9.7 1.5 pad_maximum_fusion.8
  11.3 1.5 fusion.9
  12.9 2.6 broadcast.112.clone
  15.4 1.7 constant_dynamic-update-slice_fusion.8
  17.5 2.5 collective-permute-start.1
  20.1 2.5 broadcast.112.clone.1
  22.6 1.6 constant_dynamic-update-slice_fusion.4
  26.6 17.6 %collective-permute-done.1 = bf16[512,1024]{1,0:T(8,128)(2,1)S(1)} collective-permute-done((bf16[512,1024]{1,0:T(8,128)(2,1)}, bf16[512,1024]{1,0:T(8,128)(2,1)S(1)}, u32[]{:S(2)}, u32[]{:S(2)}) %collective-permute-start.1) | collective-permute-done | bytes 1048608 | tf_op jit(solution)/shard_map/ppermute | solution.py:386
  44.3 22.3 %collective-permute-done.4 = bf16[512,1024]{1,0:T(8,128)(2,1)} collective-permute-done((bf16[512,1024]{1,0:T(8,128)(2,1)}, bf16[512,1024]{1,0:T(8,128)(2,1)}, u32[]{:S(2)}, u32[]{:S(2)}) %collective-permute-start.4) | collective-permute-done | bytes 1048608 | tf_op jit(solution)/shard_map/ppermute | solution.py:386
  73.2 2.3 constant_dynamic-update-slice_fusion.3
  75.4 2.3 constant_dynamic-update-slice_fusion.2
  77.7 2.4 constant_dynamic-update-slice_fusion.5
  80.1 2.3 constant_dynamic-update-slice_fusion.1
  82.4 7.9 %convolution_convert_fusion.1 = bf16[2048,776]{0,1:T(8,128)(2,1)} fusion(bf16[2048,1024]{1,0:T(8,128)(2,1)} %constant_dynamic-update-slice_fusion.5, bf16[1024,776]{1,0:T(8,128)(2,1)} %all-gather.3.cloned.1.call-done), kind=kOutput, calls=%fused_computation.27 | convolution fusion | flops 3256369152 | bytes 8962048 | tf_op jit(solution)/shard_map/dot_general | solution.py:476
  90.3 6.2 %copy.125.u_ref.past_ref = bf16[2048,776]{1,0:T(8,128)(2,1)} copy(bf16[2048,776]{0,1:T(8,128)(2,1)} %convolution_convert_fusion.1) | data formatting | bytes 6356992 | tf_op jit(solution)/shard_map/convert_element_type | solution.py:476
  97.7 1.4 copy.127.cumc_ref
  108.5 20.9 %scan_forward.1 = (bf16[2048,512]{1,0:T(8,128)(2,1)S(1)}, bf16[8,128,512]{2,1,0:T(8,128)(2,1)S(1)}, bf16[2048,768]{1,0:T(8,128)(2,1)S(1)}) custom-call(bf16[2048,776]{1,0:T(8,128)(2,1)} %copy.125.u_ref.past_ref, f32[4,768]{1,0:T(4,128)S(1)} %pad_maximum_fusion.12.taps_ref, f32[1,768]{1,0:T(1,128)S(1)} %broadcast_in_dim.69.bias_ref, ...), custom_call_target="tpu_custom_call" | custom-call | flops 4000000000 | bytes 8388608 | tf_op jit(solution)/shard_map/scan_forward/pallas_call | solution.py:276
  129.4 1.7 copy-done.11
  132.0 5.0 %fusion.17 = f32[2048,512]{1,0:T(8,128)S(1)} fusion(bf16[2048,1024]{1,0:T(8,128)(2,1)} %constant_dynamic-update-slice_fusion.1, bf16[1024,1024]{0,1:T(8,128)(2,1)} %all-gather.5.cloned.1.call-done), kind=kOutput, calls=%fused_computation.46 | convolution fusion | flops 2147483648 | bytes 9437184 | tf_op jit(solution)/shard_map/dot_general | solution.py:503
  137.1 8.6 %multiply_reduce_fusion.3 = (f32[2048]{0:T(1024)S(1)}, f32[2048]{0:T(1024)S(1)}, bf16[2048,512]{1,0:T(8,128)(2,1)}) fusion(bf16[2048,512]{1,0:T(8,128)(2,1)S(1)} %get-tuple-element.26, f32[2048,512]{1,0:T(8,128)S(1)} %fusion.17, f32[512]{0:T(512)S(1)} %dynamic_slice.51, bf16[2048,1024]{1,0:T(8,128)(2,1)} %constant_dynamic-update-slice_fusion.5, ...), kind=kOutput, calls=%fused_computation.18 | convolution fusion | flops 2161111040 | bytes 13649920 | tf_op jit(solution)/shard_map/dot_general | solution.py:499
  145.7 12.1 %psum.7 = f32[2,2048]{1,0:T(2,128)S(1)} all-reduce(f32[2,2048]{1,0:T(2,128)S(1)} %pad_maximum_fusion.11), channel_id=1, replica_groups=mesh['dp'=8,'tensor'=4] {'tensor'}, use_global_device_ids=true, to_apply=%region_3.4 | all-reduce | flops 4096 | bytes 32768 | tf_op jit(solution)/shard_map/psum | solution.py:510
  157.9 5.9 %convolution_convert_fusion.3 = bf16[1024,512]{0,1:T(8,128)(2,1)S(1)} fusion(bf16[2048,1024]{1,0:T(8,128)(2,1)} %constant_dynamic-update-slice_fusion.1, f32[2048]{0:T(1024)S(1)} %bitcast.91, f32[512]{0:T(512)S(1)} %dynamic_slice.51, bf16[2048,512]{1,0:T(8,128)(2,1)S(1)} %get-tuple-element.26, bf16[2048,512]{1,0:T(8,128)(2,1)} %get-tuple-element.153), kind=kOutput, calls=%fused_computation.42 | convolution fusion | flops 2158493696 | bytes 9447424 | tf_op jit(solution)/shard_map/dot_general | solution.py:31
  163.8 4.1 %fusion.1 = (bf16[2048,512]{1,0:T(8,128)(2,1)S(1)}, bf16[2048,512]{1,0:T(8,128)(2,1)S(1)}, f32[512]{0:T(512)S(1)}) fusion(bf16[2048,512]{1,0:T(8,128)(2,1)S(1)} %get-tuple-element.26, bf16[2048,512]{1,0:T(8,128)(2,1)S(1)} %copy-done.24, f32[2048]{0:T(1024)S(1)} %bitcast.94, f32[2048,512]{1,0:T(8,128)S(1)} %copy-done.21, f32[2048]{0:T(1024)S(1)} %multiply_multiply_fusion, ...), kind=kLoop, calls=%fused_computation.7 | loop fusion | flops 25165312 | bytes 12611584 | tf_op jit(solution)/shard_map/convert_element_type | solution.py:518
  167.9 5.3 %convolution_convert_fusion.4 = bf16[1024,512]{0,1:T(8,128)(2,1)S(1)} fusion(bf16[2048,1024]{1,0:T(8,128)(2,1)} %constant_dynamic-update-slice_fusion.5, bf16[2048,512]{1,0:T(8,128)(2,1)S(1)} %get-tuple-element.116), kind=kOutput, calls=%fused_computation.43 | convolution fusion | flops 2148007936 | bytes 7340032 | tf_op jit(solution)/shard_map/dot_general | solution.py:31
  173.3 1.5 pad_maximum_fusion.3
  175.7 4.8 %convolution_convert_fusion = bf16[2048,1024]{1,0:T(8,128)(2,1)} fusion(bf16[1024,1024]{0,1:T(8,128)(2,1)S(1)} %copy-done.26, f32[2048]{0:T(1024)S(1)} %bitcast.93, f32[512]{0:T(512)S(1)} %dynamic_slice.51, bf16[2048,512]{1,0:T(8,128)(2,1)S(1)} %get-tuple-element.26, bf16[2048,512]{1,0:T(8,128)(2,1)S(1)} %copy-done.24), kind=kOutput, calls=%fused_computation.25 | convolution fusion | flops 2160066560 | bytes 9447424 | tf_op jit(solution)/shard_map/dot_general | solution.py:35
  180.5 43.7 %scan_backward.1 = (bf16[2048,768]{1,0:T(8,128)(2,1)}, f32[8,768]{1,0:T(8,128)S(1)}, f32[2048,8]{1,0:T(8,128)S(1)}, f32[2048,8]{1,0:T(8,128)S(1)}, f32[8,2048]{1...) custom-call(bf16[2048,768]{1,0:T(8,128)(2,1)} %copy-done.11, ...), custom_call_target="tpu_custom_call" | custom-call | flops 10000000000 | bytes 16777216 | tf_op jit(solution)/shard_map/scan_backward/pallas_call | solution.py:328
  227.5 7.9 %fusion.15 = bf16[1024,776]{0,1:T(8,128)(2,1)} fusion(bf16[2048,1024]{1,0:T(8,128)(2,1)} %constant_dynamic-update-slice_fusion.5, bf16[2048,8]{1,0:T(8,128)(2,1)S(1)} %copy.141, bf16[2048,768]{1,0:T(8,128)(2,1)} %get-tuple-element.31), kind=kOutput, calls=%fused_computation.41 | convolution fusion | flops 3261931520 | bytes 8962048 | tf_op jit(solution)/shard_map/dot_general | solution.py:31
  235.4 3.9 %copy.147 = bf16[1024,776]{1,0:T(8,128)(2,1)} copy(bf16[1024,776]{0,1:T(8,128)(2,1)} %fusion.15) | data formatting | bytes 3178496
  239.4 2.7 copy.145
  242.2 7.1 %fusion.8 = f32[2048,1024]{1,0:T(8,128)S(1)} fusion(bf16[1024,776]{1,0:T(8,128)(2,1)} %all-gather.3.cloned.1.call-done, bf16[2048,8]{1,0:T(8,128)(2,1)S(1)} %copy.141, bf16[2048,768]{1,0:T(8,128)(2,1)} %get-tuple-element.31), kind=kOutput, calls=%fused_computation.30 | convolution fusion | flops 3261136896 | bytes 13156352 | tf_op jit(solution)/shard_map/dot_general | solution.py:35
  249.3 4.8 %multiply_reduce_fusion = (f32[1024]{0:T(1024)S(1)}, bf16[2048,1024]{1,0:T(8,128)(2,1)S(1)}) fusion(bf16[2048,1024]{1,0:T(8,128)(2,1)} %constant_dynamic-update-slice_fusion.5, f32[2048,1024]{1,0:T(8,128)S(1)} %fusion.8, bf16[2048,512]{1,0:T(8,128)(2,1)S(1)} %copy-done.19, bf16[1024,1024]{0,1:T(8,128)(2,1)S(1)} %copy-done.27), kind=kOutput, calls=%fused_computation | convolution fusion | flops 2157968384 | bytes 19927040 | tf_op jit(solution)/shard_map/dot_general | solution.py:35
  255.3 2.9 copy-done.22
  258.3 1.5 constant_dynamic-slice_fusion.3
  260.5 1.4 add_convert_fusion
  263.4 2.9 add_convert_fusion.1
  270.8 40.6 %collective-permute-done.15 = f32[14688]{0:T(1024)S(1)} collective-permute-done((f32[14688]{0:T(1024)S(1)}, f32[14688]{0:T(1024)S(1)}, u32[]{:S(2)}, u32[]{:S(2)}) %collective-permute-start.15) | collective-permute-done | bytes 58784 | tf_op jit(solution)/shard_map/ppermute | solution.py:386
  311.4 1.5 collective-permute-start.16
  312.9 2.7 collective-permute-done.16
  315.7 1.6 collective-permute-start.17
  317.3 3.9 %collective-permute-done.17 = f32[14688]{0:T(1024)S(1)} collective-permute-done((f32[14688]{0:T(1024)S(1)}, f32[14688]{0:T(1024)S(1)}, u32[]{:S(2)}, u32[]{:S(2)}) %collective-permute-start.17) | collective-permute-done | bytes 58784 | tf_op jit(solution)/shard_map/ppermute | solution.py:386
  321.3 2.5 collective-permute-start.18
  323.8 6.9 %collective-permute-done.18 = f32[14688]{0:T(1024)S(1)} collective-permute-done((f32[14688]{0:T(1024)S(1)}, f32[14688]{0:T(1024)S(1)}, u32[]{:S(2)}, u32[]{:S(2)}) %collective-permute-start.18) | collective-permute-done | bytes 58784 | tf_op jit(solution)/shard_map/ppermute | solution.py:386
  333.9 1.9 fusion.14
  337.1 4.8 %fusion.13 = (f32[512,1024]{1,0:T(8,128)}, f32[512,1024]{1,0:T(8,128)}) fusion(bf16[512,1024]{1,0:T(8,128)(2,1)S(1)} %copy-done.16, bf16[512,1024]{1,0:T(8,128)(2,1)} %param.15, bf16[512,1024]{1,0:T(8,128)(2,1)S(1)} %collective-permute-done.11, bf16[512,1024]{1,0:T(8,128)(2,1)S(1)} %collective-permute-done.9, f32[512]{0:T(512)S(1)} %broadcast_multiply_fusion.2, ...), kind=kLoop, calls=%fused_computation.35 | loop fusion | flops 10485760 | bytes 12595204 | tf_op jit(solution)/shard_map/sub | solution.py:549
  343.9 4.6 %collective-permute-done.13 = f32[128,256]{0,1:T(8,128)S(1)} collective-permute-done((f32[128,256]{0,1:T(8,128)S(1)}, f32[128,256]{0,1:T(8,128)S(1)}, u32[]{:S(2)}, u32[]{:S(2)}) %collective-permute-start.13) | collective-permute-done | bytes 131104 | tf_op jit(solution)/shard_map/ppermute | solution.py:386
  349.2 28.4 %reduce-scatter.7.cloned.1.call-done = bf16[128,1024]{1,0:T(8,128)(2,1)} async-done(((bf16[1024,1024]{1,0:T(8,128)(2,1)}), bf16[128,1024]{1,0:T(8,128)(2,1)}) %reduce-scatter.7.cloned.1.call-update) | async-done | bytes 262160
  (219 shorter events, 44.4 us)
Async XLA Ops:
  7.2 8.2 %copy-start.15 = (bf16[512,1024]{1,0:T(8,128)(2,1)S(1)}, bf16[512,1024]{1,0:T(8,128)(2,1)}, u32[]{:S(2)}) copy-start(bf16[512,1024]{1,0:T(8,128)(2,1)} %param.14) | copy-start | bytes 3145732
  7.2 8.2 %copy-start.29 = (f32[1024]{0:T(1024)S(1)}, f32[1024]{0:T(1024)}, u32[]{:S(2)}) copy-start(f32[1024]{0:T(1024)} %param.27) | copy-start | bytes 12292
  7.2 75.2 %all-gather.3.cloned.1.call-start = ((), (), s32[]{:S(2)}) async-start(), calls=%async_computation.2 | async-start | bytes 2064384 | tf_op jit(solution)/shard_map/all_gather | solution.py:460
  11.3 120.8 %all-gather.5.cloned.1.call-start = ((), (), s32[]{:S(2)}) async-start(), calls=%async_computation.3 | async-start | bytes 2359296 | tf_op jit(solution)/shard_map/all_gather | solution.py:463
  11.3 8.7 %copy-start.10 = (s32[2048]{0:T(1024)S(1)}, s32[2048]{0:T(1024)}, u32[]{:S(2)}) copy-start(s32[2048]{0:T(1024)} %param.16) | copy-start | bytes 24580
  15.4 7.2 %copy-start.23 = (bf16[512,1024]{1,0:T(8,128)(2,1)S(1)}, bf16[512,1024]{1,0:T(8,128)(2,1)}, u32[]{:S(2)}) copy-start(bf16[512,1024]{1,0:T(8,128)(2,1)} %param.15) | copy-start | bytes 3145732
  17.1 7.8 %copy-start.28 = (bf16[512,128]{1,0:T(8,128)(2,1)S(1)}, bf16[512,128]{1,0:T(8,128)(2,1)}, u32[]{:S(2)}) copy-start(bf16[512,128]{1,0:T(8,128)(2,1)} %param.20) | copy-start | bytes 393220
  17.1 54.0 %collective-permute-start = (bf16[512,1024]{1,0:T(8,128)(2,1)}, bf16[512,1024]{1,0:T(8,128)(2,1)S(1)}, u32[]{:S(2)}, u32[]{:S(2)}) collective-permute-start(bf16[512,1024]{1,0:T(8,128)(2,1)} %get-tuple-element.115), channel_id=1, source_target_pairs={{0,1},{1,0},{2,3},{3,2},{4,5},{5,4},{6,7},{7,6},{8,9},{9,8},{10,11... | collective-permute-start | bytes 3145736 | tf_op jit(solution)/shard_map/ppermute | solution.py:386
  17.5 26.7 %collective-permute-start.1 = (bf16[512,1024]{1,0:T(8,128)(2,1)}, bf16[512,1024]{1,0:T(8,128)(2,1)S(1)}, u32[]{:S(2)}, u32[]{:S(2)}) collective-permute-start(bf16[512,1024]{1,0:T(8,128)(2,1)} %get-tuple-element.115), channel_id=1, source_target_pairs={{0,2},{1,3},{2,0},{3,1},{4,6},{5,7},{6,4},{7,5},{8,10},{9,11},{10,... | collective-permute-start | bytes 3145736 | tf_op jit(solution)/shard_map/ppermute | solution.py:386
  20.1 6.0 %copy-start.30 = (f32[4,2304]{1,0:T(4,128)S(1)}, f32[4,2304]{1,0:T(4,128)}, u32[]{:S(2)}) copy-start(f32[4,2304]{1,0:T(4,128)} %param.21) | copy-start | bytes 110596
  20.1 6.2 %copy-start.31 = (f32[2304]{0:T(1024)S(1)}, f32[2304]{0:T(1024)}, u32[]{:S(2)}) copy-start(f32[2304]{0:T(1024)} %param.22) | copy-start | bytes 27652
  20.1 6.5 %slice-start.1 = ((f32[2304]{0:T(1024)}), f32[256]{0:T(256)S(1)}, s32[]{:S(2)}) async-start(f32[2304]{0:T(1024)} %param.22), calls=%async_computation.7 | async-start | bytes 2048 | tf_op jit(solution)/shard_map/slice | solution.py:486
  20.1 24.1 %copy-start.32 = (f32[32]{0:T(128)S(1)}, f32[32]{0:T(128)}, u32[]{:S(2)}) copy-start(f32[32]{0:T(128)} %param.24) | copy-start | bytes 388
  20.1 46.6 %copy-start.33 = (f32[32]{0:T(128)S(1)}, f32[32]{0:T(128)}, u32[]{:S(2)}) copy-start(f32[32]{0:T(128)} %param.23) | copy-start | bytes 388
  20.1 47.0 %copy-start.34 = (f32[32]{0:T(128)S(1)}, f32[32]{0:T(128)}, u32[]{:S(2)}) copy-start(f32[32]{0:T(128)} %param.25) | copy-start | bytes 388
  22.6 48.4 %slice-start = ((f32[4,2304]{1,0:T(4,128)}), f32[4,256]{1,0:T(4,128)S(1)}, s32[]{:S(2)}) async-start(f32[4,2304]{1,0:T(4,128)} %param.21), calls=%async_computation.6 | async-start | bytes 8192 | tf_op jit(solution)/shard_map/slice | solution.py:481
  24.2 49.0 %collective-permute-start.3 = (bf16[512,1024]{1,0:T(8,128)(2,1)}, bf16[512,1024]{1,0:T(8,128)(2,1)}, u32[]{:S(2)}, u32[]{:S(2)}) collective-permute-start(bf16[512,1024]{1,0:T(8,128)(2,1)} %get-tuple-element.109), channel_id=1, source_target_pairs={{0,1},{1,0},{2,3},{3,2},{4,5},{5,4},{6,7},{7,6},{8,9},{9,8},{10,11... | collective-permute-start | bytes 3145736 | tf_op jit(solution)/shard_map/ppermute | solution.py:386
  24.4 42.2 %collective-permute-start.4 = (bf16[512,1024]{1,0:T(8,128)(2,1)}, bf16[512,1024]{1,0:T(8,128)(2,1)}, u32[]{:S(2)}, u32[]{:S(2)}) collective-permute-start(bf16[512,1024]{1,0:T(8,128)(2,1)} %get-tuple-element.109), channel_id=1, source_target_pairs={{0,2},{1,3},{2,0},{3,1},{4,6},{5,7},{6,4},{7,5},{8,10},{9,11},{10,... | collective-permute-start | bytes 3145736 | tf_op jit(solution)/shard_map/ppermute | solution.py:386
  25.6 310.2 %reduce-scatter.9.cloned.1.call-start = ((), (), s32[]{:S(2)}) async-start(), calls=%async_computation.5 | async-start | bytes 2064384
  44.2 33.5 %collective-permute-start.2 = (bf16[512,1024]{1,0:T(8,128)(2,1)S(1)}, bf16[512,1024]{1,0:T(8,128)(2,1)}, u32[]{:S(2)}, u32[]{:S(2)}) collective-permute-start(bf16[512,1024]{1,0:T(8,128)(2,1)S(1)} %collective-permute-done.1), channel_id=1, source_target_pairs={{0,1},{1,0},{2,3},{3,2},{4,5},{5,4},{6,7},{7,6},{8,9},{9,8},{10,11... | collective-permute-start | bytes 3145736 | tf_op jit(solution)/shard_map/ppermute | solution.py:386
  66.6 13.5 %collective-permute-start.5 = (bf16[512,1024]{1,0:T(8,128)(2,1)}, bf16[512,1024]{1,0:T(8,128)(2,1)}, u32[]{:S(2)}, u32[]{:S(2)}) collective-permute-start(bf16[512,1024]{1,0:T(8,128)(2,1)} %collective-permute-done.4), channel_id=1, source_target_pairs={{0,1},{1,0},{2,3},{3,2},{4,5},{5,4},{6,7},{7,6},{8,9},{9,8},{10,11... | collective-permute-start | bytes 3145736 | tf_op jit(solution)/shard_map/ppermute | solution.py:386
  132.0 5.1 %copy-start.25 = (bf16[1024,1024]{0,1:T(8,128)(2,1)S(1)}, bf16[1024,1024]{0,1:T(8,128)(2,1)}, u32[]{:S(2)}) copy-start(bf16[1024,1024]{0,1:T(8,128)(2,1)} %all-gather.5.cloned.1.call-done) | copy-start | bytes 6291460
  137.1 8.6 %copy-start.20 = (f32[2048,512]{1,0:T(8,128)}, f32[2048,512]{1,0:T(8,128)S(1)}, u32[]{:S(2)}) copy-start(f32[2048,512]{1,0:T(8,128)S(1)} %fusion.17) | copy-start | bytes 12582916
  157.9 5.9 %copy-start.21 = (f32[2048,512]{1,0:T(8,128)S(1)}, f32[2048,512]{1,0:T(8,128)}, u32[]{:S(2)}) copy-start(f32[2048,512]{1,0:T(8,128)} %copy-done.20) | copy-start | bytes 12582916
  157.9 5.9 %copy-start.24 = (bf16[2048,512]{1,0:T(8,128)(2,1)S(1)}, bf16[2048,512]{1,0:T(8,128)(2,1)}, u32[]{:S(2)}) copy-start(bf16[2048,512]{1,0:T(8,128)(2,1)} %get-tuple-element.153) | copy-start | bytes 6291460
  167.9 5.4 %copy-start.18 = (bf16[2048,512]{1,0:T(8,128)(2,1)}, bf16[2048,512]{1,0:T(8,128)(2,1)S(1)}, u32[]{:S(2)}) copy-start(bf16[2048,512]{1,0:T(8,128)(2,1)S(1)} %get-tuple-element.116) | copy-start | bytes 6291460
  175.7 4.8 %copy-start.6 = (f32[8,256,8]{2,1,0:T(8,128)S(1)}, f32[8,256,8]{2,1,0:T(8,128)}, u32[]{:S(2)}) copy-start(f32[8,256,8]{2,1,0:T(8,128)} %copy.123) | copy-start | bytes 196612
  175.7 4.8 %copy-start.8 = (f32[8,256,8]{2,1,0:T(8,128)S(1)}, f32[8,256,8]{2,1,0:T(8,128)}, u32[]{:S(2)}) copy-start(f32[8,256,8]{2,1,0:T(8,128)} %copy.124) | copy-start | bytes 196612
  175.7 4.8 %copy-start.9 = (f32[8,256,8]{2,1,0:T(8,128)S(1)}, f32[8,256,8]{2,1,0:T(8,128)}, u32[]{:S(2)}) copy-start(f32[8,256,8]{2,1,0:T(8,128)} %copy.131) | copy-start | bytes 196612
  175.7 4.8 %copy-start.13 = (bf16[8,128,512]{2,1,0:T(8,128)(2,1)S(1)}, bf16[8,128,512]{2,1,0:T(8,128)(2,1)}, u32[]{:S(2)}) copy-start(bf16[8,128,512]{2,1,0:T(8,128)(2,1)} %copy-done.12) | copy-start | bytes 3145732
  239.3 138.3 %reduce-scatter.7.cloned.1.call-start = ((), (), s32[]{:S(2)}) async-start(), calls=%async_computation.4 | async-start | bytes 2359296
  242.1 7.2 %copy-start.19 = (bf16[2048,512]{1,0:T(8,128)(2,1)S(1)}, bf16[2048,512]{1,0:T(8,128)(2,1)}, u32[]{:S(2)}) copy-start(bf16[2048,512]{1,0:T(8,128)(2,1)} %copy-done.18) | copy-start | bytes 6291460
  242.2 7.2 %copy-start.27 = (bf16[1024,1024]{0,1:T(8,128)(2,1)S(1)}, bf16[1024,1024]{0,1:T(8,128)(2,1)}, u32[]{:S(2)}) copy-start(bf16[1024,1024]{0,1:T(8,128)(2,1)} %all-gather.5.cloned.1.call-done) | copy-start | bytes 6291460
  254.2 6.3 %copy-start.14 = (bf16[2048,1024]{1,0:T(8,128)(2,1)}, bf16[2048,1024]{1,0:T(8,128)(2,1)S(1)}, u32[]{:S(2)}) copy-start(bf16[2048,1024]{1,0:T(8,128)(2,1)S(1)} %get-tuple-element.120) | copy-start | bytes 12582916
  255.3 5.1 %collective-permute-start.10 = (bf16[512,1024]{1,0:T(8,128)(2,1)S(1)}, bf16[512,1024]{1,0:T(8,128)(2,1)S(1)}, u32[]{:S(2)}, u32[]{:S(2)}) collective-permute-start(bf16[512,1024]{1,0:T(8,128)(2,1)S(1)} %get-tuple-element.122), channel_id=1, source_target_pairs={{0,1},{1,0},{2,3},{3,2},{4,5},{5,4},{6,7},{7,6},{8,9},{9,8},{10,11... | collective-permute-start | bytes 3145736 | tf_op jit(solution)/shard_map/ppermute | solution.py:386
  259.8 74.1 %copy-start.16 = (bf16[512,1024]{1,0:T(8,128)(2,1)S(1)}, bf16[512,1024]{1,0:T(8,128)(2,1)}, u32[]{:S(2)}) copy-start(bf16[512,1024]{1,0:T(8,128)(2,1)} %param.14) | copy-start | bytes 3145732
  259.8 3.6 collective-permute-start.7
  259.8 74.0 %collective-permute-start.9 = (bf16[512,1024]{1,0:T(8,128)(2,1)}, bf16[512,1024]{1,0:T(8,128)(2,1)S(1)}, u32[]{:S(2)}, u32[]{:S(2)}) collective-permute-start(bf16[512,1024]{1,0:T(8,128)(2,1)} %get-tuple-element.121), channel_id=1, source_target_pairs={{0,1},{1,0},{2,3},{3,2},{4,5},{5,4},{6,7},{7,6},{8,9},{9,8},{10,11... | collective-permute-start | bytes 3145736 | tf_op jit(solution)/shard_map/ppermute | solution.py:386
  260.4 76.7 %collective-permute-start.6 = (bf16[512,1024]{1,0:T(8,128)(2,1)}, bf16[512,1024]{1,0:T(8,128)(2,1)}, u32[]{:S(2)}, u32[]{:S(2)}) collective-permute-start(bf16[512,1024]{1,0:T(8,128)(2,1)} %get-tuple-element.123), channel_id=1, source_target_pairs={{0,1},{1,0},{2,3},{3,2},{4,5},{5,4},{6,7},{7,6},{8,9},{9,8},{10,11... | collective-permute-start | bytes 3145736 | tf_op jit(solution)/shard_map/ppermute | solution.py:386
  261.9 72.0 %collective-permute-start.11 = (bf16[512,1024]{1,0:T(8,128)(2,1)}, bf16[512,1024]{1,0:T(8,128)(2,1)S(1)}, u32[]{:S(2)}, u32[]{:S(2)}) collective-permute-start(bf16[512,1024]{1,0:T(8,128)(2,1)} %add_convert_fusion), channel_id=1, source_target_pairs={{0,2},{1,3},{2,0},{3,1},{4,6},{5,7},{6,4},{7,5},{8,10},{9,11},{10,... | collective-permute-start | bytes 3145736 | tf_op jit(solution)/shard_map/ppermute | solution.py:386
  266.3 70.7 %collective-permute-start.8 = (bf16[512,1024]{1,0:T(8,128)(2,1)}, bf16[512,1024]{1,0:T(8,128)(2,1)}, u32[]{:S(2)}, u32[]{:S(2)}) collective-permute-start(bf16[512,1024]{1,0:T(8,128)(2,1)} %add_convert_fusion.1), channel_id=1, source_target_pairs={{0,2},{1,3},{2,0},{3,1},{4,6},{5,7},{6,4},{7,5},{8,10},{9,11},{10,... | collective-permute-start | bytes 3145736 | tf_op jit(solution)/shard_map/ppermute | solution.py:386
  268.5 1.3 collective-permute-start.14
  269.8 41.5 %collective-permute-start.15 = (f32[14688]{0:T(1024)S(1)}, f32[14688]{0:T(1024)S(1)}, u32[]{:S(2)}, u32[]{:S(2)}) collective-permute-start(f32[14688]{0:T(1024)S(1)} %add.221), channel_id=1, source_target_pairs={{0,2},{1,3},{2,0},{3,1},{4,6},{5,7},{6,4},{7,5},{8,10},{9,11},{10,... | collective-permute-start | bytes 176264 | tf_op jit(solution)/shard_map/ppermute | solution.py:386
  311.4 4.3 %collective-permute-start.16 = (f32[14688]{0:T(1024)S(1)}, f32[14688]{0:T(1024)S(1)}, u32[]{:S(2)}, u32[]{:S(2)}) collective-permute-start(f32[14688]{0:T(1024)S(1)} %add.222), channel_id=1, source_target_pairs={{0,4},{4,0},{8,12},{12,8},{16,20},{20,16},{24,28},{28,24},{1,5},{5... | collective-permute-start | bytes 176264 | tf_op jit(solution)/shard_map/ppermute | solution.py:386
  315.7 5.6 %collective-permute-start.17 = (f32[14688]{0:T(1024)S(1)}, f32[14688]{0:T(1024)S(1)}, u32[]{:S(2)}, u32[]{:S(2)}) collective-permute-start(f32[14688]{0:T(1024)S(1)} %add.223), channel_id=1, source_target_pairs={{0,8},{4,12},{8,0},{12,4},{16,24},{20,28},{24,16},{28,20},{1,9},{5... | collective-permute-start | bytes 176264 | tf_op jit(solution)/shard_map/ppermute | solution.py:386
  321.3 9.4 %collective-permute-start.18 = (f32[14688]{0:T(1024)S(1)}, f32[14688]{0:T(1024)S(1)}, u32[]{:S(2)}, u32[]{:S(2)}) collective-permute-start(f32[14688]{0:T(1024)S(1)} %add.224), channel_id=1, source_target_pairs={{0,16},{4,20},{8,24},{12,28},{16,0},{20,4},{24,8},{28,12},{1,17},{... | collective-permute-start | bytes 176264 | tf_op jit(solution)/shard_map/ppermute | solution.py:386
  337.0 5.5 %collective-permute-start.12 = (f32[128,256]{0,1:T(8,128)S(1)}, f32[128,256]{0,1:T(8,128)S(1)}, u32[]{:S(2)}, u32[]{:S(2)}) collective-permute-start(f32[128,256]{0,1:T(8,128)S(1)} %slice.161), channel_id=1, source_target_pairs={{0,1},{1,0},{2,3},{3,2},{4,5},{5,4},{6,7},{7,6},{8,9},{9,8},{10,11... | collective-permute-start | bytes 393224 | tf_op jit(solution)/shard_map/ppermute | solution.py:386
  342.5 5.9 %collective-permute-start.13 = (f32[128,256]{0,1:T(8,128)S(1)}, f32[128,256]{0,1:T(8,128)S(1)}, u32[]{:S(2)}, u32[]{:S(2)}) collective-permute-start(f32[128,256]{0,1:T(8,128)S(1)} %slice_add_fusion), channel_id=1, source_target_pairs={{0,2},{1,3},{2,0},{3,1},{4,6},{5,7},{6,4},{7,5},{8,10},{9,11},{10,... | collective-permute-start | bytes 393224 | tf_op jit(solution)/shard_map/ppermute | solution.py:386
  (12 other events, 32.4 us)
Sparse Core Ops, SparseCore 0:
  11.4 48.9 all-gather.2
  63.0 49.9 all-gather.4
  239.4 66.5 reduce-scatter.8
  309.9 67.7 reduce-scatter.6
